TPU v7x, 128 devices: a whole 4x4x4 slice. The times are simulated.
128 devices in a mesh: ny: 8 (over x, core), nx: 16 (over y, z).
Axes of the slice: x: 4, y: 4, z: 4, core: 2. Of those that a mesh axis runs over, the one named last changes fastest.
Arguments:
- elevation: float32 [1152, 18432], P('ny', 'nx'), may hold values from -6 to 6
- flux_x: float32 [1152, 18432], P('ny', 'nx'), may hold values from -3 to 3
- flux_y: float32 [1152, 18432], P('ny', 'nx'), may hold values from -3 to 3
- depth: float32 [1152, 18432], P('ny', 'nx'), may hold values from 0.5 to 2
- wet_mask: int32 [4, 1152, 18432], P(None, 'ny', 'nx'), may hold values 0 or 1
- shifts: int32 [4, 2], replicated, may hold values from 0 to 9, as said below
- parent_vals: float32 [4, 32768, 128], P(None, ('ny', 'nx')), may hold values from -3 to 3
- row_dest: int32 [4, 32768], P(None, ('ny', 'nx')), may hold values from 0 to 127, as said below
- row_coarse: int32 [4, 32768], P(None, ('ny', 'nx')), may hold values from 0 to 15
- edge_owner: int32 [4, 8], P(None, 'ny'), may hold values from 0 to 15
- edge_panels: float32 [4, 16, 1152], P(None, 'nx', 'ny'), may hold values from -8 to 8
Outputs:
- elevation_out: float32 [1152, 18432], P('ny', 'nx')
- flux_x_out: float32 [1152, 18432], P('ny', 'nx')
- flux_y_out: float32 [1152, 18432], P('ny', 'nx')
Inputs may be any that keep to these rules, and one draw needn't show every extreme that they name: In every draw some step shifts the rows by 9 and some step shifts the columns by 9. `row_dest`: in each step, of the 256 rows of one device at most 8 name any one owner; in each step one owner is named by exactly 8 rows of every device.
All inputs are finite; a program needn't handle non-finite values. No bound on the sum of `wet_mask` on one device may be relied on, other than what follows from the above.
Results may differ from a plain program's by a relative error of at most 0.00014.
Values sent between devices are 32-bit elements; how exact they have to be, the bound alone decides.
No kernel may reach another device: no remote copies, remote signals or barrier semaphores. Data moves between devices by JAX's collectives and lax.ppermute only.
A program may use at most 128 MiB of HBM per device.

v0:
```python
import functools

import jax
import jax.numpy as jnp
from jax import lax
from jax.experimental import pallas as pl
from jax.experimental.pallas import tpu as pltpu
from jax.sharding import PartitionSpec as P

RATIO = 9
STEPS = 4
CAP = 8
COARSE = 16
LANES = 128
ROWS, COLS = 144, 1152
FR, FC = 152, 1280
ROW0, COL0 = 4, 40
NHALO = 40
WIDTHS = (32, 24, 16, 8)
N_E, N_B, N_M = 0, 120, (152, 184, 208, 224)
N_ROWS, S_ROWS = 232, 64
CHUNK = 40
KTILE = COLS // LANES
E_PLACE = ((0, 0), (0, 40), (0, 80), (1, 0), (1, 64), (2, 0), (2, 32), (1, 32), (1, 88), (2, 16), (2, 40))
E_WIDTH = (40, 40, 40, 32, 24, 16, 8, 32, 24, 16, 8)

F32, BF16, I32 = jnp.float32, jnp.bfloat16, jnp.int32
VMEM = pl.BlockSpec(memory_space=pltpu.VMEM)
SMEM = pl.BlockSpec(memory_space=pltpu.SMEM)


def iota(shape, dim):
    return lax.broadcasted_iota(I32, shape, dim)


def left_over(shifts_ref, step, dim):
    total = jnp.int32(0)
    for later in range(STEPS):
        total += jnp.where(later > step, shifts_ref[later, dim], 0)
    return total


def halves(x):
    high = x.astype(BF16)
    return high, (x - high.astype(F32)).astype(BF16)


def dot(a, b, dims=((1,), (0,))):
    return lax.dot_general(a, b, (dims, ((), ())), preferred_element_type=F32)


def pack_kernel(dest_ref, dest_col_ref, coarse_col_ref, vals_ref, edge_ref, out_ref):
    owners = out_ref.shape[0]
    count = dest_ref.shape[1]
    before = iota((count, count), 0) < iota((count, count), 1)
    lane = iota((count, LANES), 1)
    place_row = iota((owners * CAP, count), 0)
    meta = jnp.zeros((owners * CAP, LANES), F32)
    for s in range(STEPS):
        dest = dest_ref[s : s + 1, :]
        same = (dest_col_ref[:, s : s + 1] == dest) & before
        slot = jnp.sum(jnp.where(same, 1.0, 0.0), axis=0, keepdims=True).astype(I32)
        hits = jnp.where(place_row == dest * CAP + slot, 1.0, 0.0).astype(BF16)
        high, low = halves(vals_ref[s])
        target = jnp.where(lane == s, coarse_col_ref[:, s : s + 1] + 1, 0).astype(F32).astype(BF16)
        out_ref[:, s * CAP : (s + 1) * CAP, :] = (dot(hits, high) + dot(hits, low)).reshape(
            owners, CAP, LANES
        )
        meta += dot(hits, target)
    out_ref[:, STEPS * CAP :, :] = meta.reshape(owners, CAP, LANES) + edge_ref[...][None]


def receive_kernel(got_ref, coarse_ref, edge_ref):
    sources = got_ref.shape[0]
    meta = got_ref[:, STEPS * CAP :, :].reshape(sources * CAP, LANES)
    lane = iota((sources * CAP, LANES), 1)
    for s in range(STEPS):
        target = meta[:, s : s + 1].astype(I32) - 1
        hits = jnp.where(lane == target, 1.0, 0.0).astype(BF16)
        high, low = halves(got_ref[:, s * CAP : (s + 1) * CAP, :].reshape(sources * CAP, LANES))
        both = ((0,), (0,))
        coarse_ref[s] = (dot(hits, high, both) + dot(hits, low, both))[:COARSE]
    row_block, col_groups = lax.axis_index("ny"), lax.axis_size("nx")
    for k in range(3):
        block = jnp.clip(row_block + k - 1, 0, lax.axis_size("ny") - 1)
        edge_ref[k] = jnp.sum(
            got_ref[pl.ds(block * col_groups, col_groups), STEPS * CAP :, :], axis=0
        )


def edge_flags():
    row_block, col_block = lax.axis_index("ny"), lax.axis_index("nx")
    south = jnp.where(row_block == 0, 0.0, 1.0).astype(F32)
    north = jnp.where(row_block == lax.axis_size("ny") - 1, 0.0, 1.0).astype(F32)
    west = jnp.where(col_block == 0, 0.0, 1.0).astype(F32)
    east = jnp.where(col_block == lax.axis_size("nx") - 1, 0.0, 1.0).astype(F32)
    return south, north, west, east


def fill_rows(tall_ref, own, south_ref, field, north_ref, north_at, width, flags):
    south, north = flags[0], flags[1]
    tall_ref[0:8, :] = south_ref[8 * field : 8 * field + 8, :] * south
    tall_ref[8 : 8 + ROWS, :] = own
    tall_ref[8 + ROWS : 8 + ROWS + width, :] = north_ref[north_at : north_at + width, :] * north


def window(tall_ref, row_shift, lanes):
    start = row_shift + ROW0
    base = pl.multiple_of((start >> 3) << 3, 8)
    tall = tall_ref[pl.ds(base, FR + 8), lanes]
    return pltpu.roll(tall, FR + 8 - (start & 7), 0)[:FR]


def pack_sides_kernel(
    shifts_ref, e_ref, u_ref, v_ref, b_ref, m_ref, north_ref, south_ref, out_ref, tall_ref
):
    side = pl.program_id(0)
    flags = edge_flags()
    lane = iota((FR, LANES), 1)
    tall_ref[...] = jnp.zeros_like(tall_ref)
    fields = []
    for f, ref in enumerate((e_ref, u_ref, v_ref)):
        fill_rows(tall_ref, ref[...], south_ref, f, north_ref, N_E + NHALO * f, NHALO, flags)
        fields.append(window(tall_ref, left_over(shifts_ref, -1, 0), slice(None)))
    fill_rows(tall_ref, b_ref[...], south_ref, 3, north_ref, N_B, WIDTHS[0], flags)
    for s in range(STEPS):
        fields.append(window(tall_ref, left_over(shifts_ref, s, 0), slice(None)))
    for s in range(STEPS):
        own = m_ref[s].astype(F32)
        fill_rows(tall_ref, own, south_ref, 4 + s, north_ref, N_M[s], WIDTHS[s], flags)
        fields.append(window(tall_ref, left_over(shifts_ref, s, 0), slice(None)))

    @pl.when(side == 0)
    def _():
        tiles = [jnp.zeros((FR, LANES), F32)] * 3
        for x, (tile, at), width in zip(fields, E_PLACE, E_WIDTH):
            moved = pltpu.roll(x, at, 1) if at else x
            tiles[tile] = jnp.where((lane >= at) & (lane < at + width), moved, tiles[tile])
        for k in range(3):
            out_ref[0, k] = tiles[k]

    @pl.when(side == 1)
    def _():
        tile = jnp.zeros((FR, LANES), F32)
        for f, x in enumerate(fields):
            moved = pltpu.roll(x, 8 * f + 8, 1)
            tile = jnp.where((lane >= 8 * f) & (lane < 8 * f + 8), moved, tile)
        out_ref[0, 0] = tile
        out_ref[0, 1] = tile
        out_ref[0, 2] = tile


def side_tiles(east_ref, west_ref, which, flags):
    tile, at = E_PLACE[which]
    right = east_ref[tile]
    if at:
        right = pltpu.roll(right, LANES - at, 1)
    left = pltpu.roll(west_ref[...], 120 - 8 * which, 1)
    return left * flags[2], right * flags[3]


def framed(tall_ref, row_shift, col_shift, left, right, write):
    lane = iota((FR, LANES), 1)
    turn = 128 - COL0 + col_shift
    amount = LANES - turn
    keep = lane < amount
    this = pltpu.roll(left, amount, 1)
    for k in range(FC // LANES):
        lanes = slice(k * LANES, (k + 1) * LANES)
        following = window(tall_ref, row_shift, lanes) if k < KTILE else right
        following = pltpu.roll(following, amount, 1)
        write(k, jnp.where(keep, this, following))
        this = following


def divide_18(n):
    return (n * 3641) >> 16


def prepare_kernel(
    shifts_ref, e_ref, u_ref, v_ref, b_ref, m_ref, north_ref, south_ref, east_ref, west_ref,
    state_ref, coef_ref, cols_ref, tall_ref, wet_ref, deep_ref, side_ref,
):
    s = pl.program_id(0)
    flags = edge_flags()
    is_west = lax.axis_index("nx") == 0

    @pl.when(s == 0)
    def _():
        tall_ref[...] = jnp.zeros_like(tall_ref)
        wet_ref[...] = jnp.zeros_like(wet_ref)
        deep_ref[...] = jnp.zeros_like(deep_ref)
        row_all, col_all = left_over(shifts_ref, -1, 0), left_over(shifts_ref, -1, 1)
        for f, ref in enumerate((e_ref, u_ref, v_ref)):
            fill_rows(tall_ref, ref[...], south_ref, f, north_ref, N_E + NHALO * f, NHALO, flags)

            def write(k, x, f=f):
                state_ref[f, :, k * LANES : (k + 1) * LANES] = x

            left, right = side_tiles(east_ref, west_ref, f, flags)
            framed(tall_ref, row_all, col_all, left, right, write)

    row_left, col_left = left_over(shifts_ref, s, 0), left_over(shifts_ref, s, 1)
    for step in range(STEPS):

        @pl.when(s == step)
        def _(step=step):
            side_ref[0], side_ref[1] = side_tiles(east_ref, west_ref, 3 + step, flags)
            side_ref[2], side_ref[3] = side_tiles(east_ref, west_ref, 7 + step, flags)

    fill_rows(tall_ref, b_ref[...], south_ref, 3, north_ref, N_B, WIDTHS[0], flags)

    def write_depth(k, x):
        deep_ref[0:FR, k * LANES : (k + 1) * LANES] = x

    framed(tall_ref, row_left, col_left, side_ref[0], side_ref[1], write_depth)

    for step in range(STEPS):

        @pl.when(s == step)
        def _(step=step):
            own = m_ref[0].astype(F32)
            fill_rows(
                tall_ref, own, south_ref, 4 + step, north_ref, N_M[step], WIDTHS[step], flags
            )

    row = iota((FR, LANES), 0)
    nest_row = lax.axis_index("ny") * ROWS + row + row_left - ROW0
    in_nest = (nest_row >= 0) & (nest_row < ROWS * lax.axis_size("ny"))
    lane = iota((FR, LANES), 1)
    ghost = in_nest & (lane == COL0 - 1 - col_left) & is_west

    def write_wet(k, x):
        coef_ref[0, 4, :, k * LANES : (k + 1) * LANES] = x
        wet_ref[0:FR, k * LANES : (k + 1) * LANES] = jnp.where(ghost, 1.0, x) if k == 0 else x

    framed(tall_ref, row_left, col_left, side_ref[2], side_ref[3], write_wet)

    for at in range(0, FR, 8):
        tile, above = slice(at, at + 8), slice(at + 1, at + 9)
        wet, deep = wet_ref[tile, :], deep_ref[tile, :]
        open_x = 0.0625 * wet * pltpu.roll(wet, FC - 1, 1)
        open_y = 0.0625 * wet * wet_ref[above, :]
        coef_ref[0, 0, tile, :] = open_x
        coef_ref[0, 1, tile, :] = open_x * (deep + pltpu.roll(deep, FC - 1, 1))
        coef_ref[0, 2, tile, :] = open_y
        coef_ref[0, 3, tile, :] = open_y * (deep + deep_ref[above, :])

    col = iota((1, FC), 1) + col_left - COL0
    inside = jnp.where(col < 0, col + COLS, jnp.where(col >= COLS, col - COLS, col))
    numerator = 2 * inside + 1 - RATIO
    lower = jnp.clip(divide_18(numerator + 18) - 1, 0, LANES - 2)
    weight = jnp.clip(numerator - 18 * lower, 0, 18)
    first = lower + jnp.where((col < 0) | (col >= COLS), LANES, 0)
    for part in range(2):
        place = iota((LANES, FC), 0) + part * LANES
        cols_ref[0, part * LANES : (part + 1) * LANES, :] = jnp.where(
            place == first, 18 - weight, jnp.where(place == first + 1, weight, 0)
        ).astype(F32).astype(BF16)


def steps_kernel(
    shifts_ref, state_ref, coef_ref, cols_ref, own_ref, east_ref, west_ref, edge_ref,
    e_out, u_out, v_out, cur, rise, flow,
):
    s = pl.program_id(0)
    row_left, col_left = left_over(shifts_ref, s, 0), left_over(shifts_ref, s, 1)
    is_west = lax.axis_index("nx") == 0
    east = jnp.where(lax.axis_index("nx") == lax.axis_size("nx") - 1, 0.0, 1.0).astype(F32)

    @pl.when(s == 0)
    def _():
        for f in range(3):
            cur[f, 0:8, :] = jnp.zeros((8, FC), F32)
            cur[f, 8 : 8 + FR, :] = state_ref[f]
            cur[f, 8 + FR :, :] = jnp.zeros((8, FC), F32)
            flow[f] = jnp.zeros((16, FC), F32)

    i = iota((FR, 1), 0) + row_left - ROW0
    block = jnp.where(i < 0, 0, jnp.where(i >= ROWS, 2, 1))
    inside = i - (block - 1) * ROWS
    numerator = 2 * inside + 1 - RATIO
    lower = jnp.clip(divide_18(numerator + 18) - 1, 0, COARSE - 2)
    weight = jnp.clip(numerator - 18 * lower, 0, 18)
    first = lower + 16 * block - 8
    place = iota((FR, 32), 1)
    rows = jnp.where(place == first, 18 - weight, jnp.where(place == first + 1, weight, 0))
    rows = rows.astype(F32).astype(BF16)
    side = jnp.where(iota((32, LANES), 1) < 64, east_ref[0] * east, west_ref[0])
    total = 0.0
    parts = []
    for x in (own_ref[0], side):
        high, low = halves(x)
        parts.append(dot(rows, high) + dot(rows, low))
    section = jnp.concatenate(parts, axis=1) * (1.0 / 324.0)
    high, low = halves(section)
    rise[...] = dot(high, cols_ref[0]) + dot(low, cols_ref[0])

    half = jnp.where(inside >= 72, 1, 0)
    pick = jnp.where(iota((FR, 24), 1) == 8 * block + 2 * s + half, 1.0, 0.0).astype(BF16)
    high, low = halves(edge_ref[...].reshape(24, LANES))
    line = dot(pick, high) + dot(pick, low)
    lane = iota((FR, LANES), 1)
    edge = jnp.sum(jnp.where(lane == 8 + inside - 72 * half, line, 0.0), axis=1, keepdims=True)
    ghost = (lane == COL0 - 1 - col_left) & is_west

    cur[0, 8 : 8 + FR, :] += rise[...]
    cur[0, 8 : 8 + FR, 0:LANES] = jnp.where(ghost, edge, cur[0, 8 : 8 + FR, 0:LANES])
    cur[1, 8 : 8 + FR, 0:LANES] = jnp.where(ghost, 0.0, cur[1, 8 : 8 + FR, 0:LANES])
    cur[2, 8 : 8 + FR, 0:LANES] = jnp.where(ghost, 0.0, cur[2, 8 : 8 + FR, 0:LANES])

    def eastern(x):
        return pltpu.roll(x, FC - 1, 1)

    def net_x(x):
        return x - pltpu.roll(x, 1, 1)

    for at in range(0, FR, 8):
        own, above, tile = slice(at + 8, at + 16), slice(at + 9, at + 17), slice(at, at + 8)
        E, U, V = cur[0, own, :], cur[1, own, :], cur[2, own, :]
        bx, cx, by, cy = (coef_ref[0, k, tile, :] for k in range(4))
        inner = coef_ref[0, 4, tile, :]
        Ee, Ue, Ve = eastern(E), eastern(U), eastern(V)
        new_e = E - net_x(bx * (2.0 * (U + Ue) - (Ee - E)))
        new_u = U - net_x(cx * (E + Ee) - bx * (Ue - U))
        new_v = V + net_x(bx * (Ve - V))
        En, Un, Vn = cur[0, above, :], cur[1, above, :], cur[2, above, :]
        north = (
            by * (2.0 * (V + Vn) - (En - E)),
            by * (Un - U),
            cy * (E + En) - by * (Vn - V),
        )
        net = []
        for f in range(3):
            flow[f, 7:8, :] = flow[f, 15:16, :]
            flow[f, 8:16, :] = north[f]
            net.append(north[f] - flow[f, 7:15, :])
        cur[0, own, :] = new_e - net[0]
        cur[1, own, :] = inner * (new_u + net[1])
        cur[2, own, :] = inner * (new_v - net[2])

    @pl.when(s == STEPS - 1)
    def _():
        lane8 = iota((ROWS, LANES), 1)
        for f, ref in enumerate((e_out, u_out, v_out)):
            this = pltpu.roll(cur[f, 8 + ROW0 : 8 + ROW0 + ROWS, 0:LANES], LANES - COL0, 1)
            for k in range(KTILE):
                following = cur[f, 8 + ROW0 : 8 + ROW0 + ROWS, (k + 1) * LANES : (k + 2) * LANES]
                following = pltpu.roll(following, LANES - COL0, 1)
                ref[:, k * LANES : (k + 1) * LANES] = jnp.where(
                    lane8 < LANES - COL0, this, following
                )
                this = following


def ring(value, axis, by):
    count = lax.axis_size(axis)
    return lax.ppermute(value, axis, [(i, (i + by) % count) for i in range(count)])


def limits(mib, **more):
    return pltpu.CompilerParams(vmem_limit_bytes=mib * 1024 * 1024, **more)


def local(
    elevation, flux_x, flux_y, depth, wet_mask, shifts, parent_vals, row_dest, row_coarse,
    edge_owner, edge_panels,
):
    owners = lax.axis_size("ny") * lax.axis_size("nx")
    sds = jax.ShapeDtypeStruct
    wet = [wet_mask[s] for s in range(STEPS)]

    north_message = jnp.concatenate(
        [x[:NHALO] for x in (elevation, flux_x, flux_y)]
        + [depth[: WIDTHS[0]]]
        + [x[:w].astype(F32) for x, w in zip(wet, WIDTHS)]
    )
    south_message = jnp.concatenate(
        [x[-8:] for x in (elevation, flux_x, flux_y, depth)] + [x[-8:].astype(F32) for x in wet]
    )
    from_north = ring(north_message, "ny", -1)
    from_south = ring(south_message, "ny", 1)

    panel = jnp.where(edge_owner == lax.axis_index("nx"), edge_panels[:, 0, :], 0.0)
    panel = jnp.pad(panel.reshape(2 * STEPS, 72), ((0, 0), (8, 48)))
    send = pl.pallas_call(
        pack_kernel,
        out_shape=sds((owners, CHUNK, LANES), F32),
        in_specs=[VMEM] * 5,
        out_specs=VMEM,
        compiler_params=limits(40),
        cost_estimate=pl.CostEstimate(flops=800_000_000, bytes_accessed=3_200_000, transcendentals=0),
        name="pack_rows",
    )(row_dest, row_dest.T, row_coarse.T, parent_vals, panel)
    got = lax.all_to_all(send, ("ny", "nx"), split_axis=0, concat_axis=0, tiled=True)

    last = KTILE - 1
    pick = lambda g: (0, g * last)
    sides = pl.pallas_call(
        pack_sides_kernel,
        out_shape=sds((2, 3, FR, LANES), F32),
        grid=(2,),
        in_specs=[SMEM]
        + [pl.BlockSpec((ROWS, LANES), pick)] * 4
        + [pl.BlockSpec((STEPS, ROWS, LANES), lambda g: (0, 0, g * last))]
        + [pl.BlockSpec((N_ROWS, LANES), pick), pl.BlockSpec((S_ROWS, LANES), pick)],
        out_specs=pl.BlockSpec((1, 3, FR, LANES), lambda g: (g, 0, 0, 0)),
        scratch_shapes=[pltpu.VMEM((16 + ROWS + NHALO, LANES), F32)],
        compiler_params=limits(32),
        cost_estimate=pl.CostEstimate(flops=8_000_000, bytes_accessed=2_500_000, transcendentals=0),
        name="pack_sides",
    )(shifts, elevation, flux_x, flux_y, depth, wet_mask, from_north, from_south)
    from_east = ring(sides[0], "nx", -1)
    from_west = ring(sides[1, 0], "nx", 1)

    whole = lambda *shape: pl.BlockSpec(shape, lambda g: (0,) * len(shape))
    state, coef, cols = pl.pallas_call(
        prepare_kernel,
        out_shape=(
            sds((3, FR, FC), F32),
            sds((STEPS, 5, FR, FC), F32),
            sds((STEPS, 2 * LANES, FC), BF16),
        ),
        grid=(STEPS,),
        in_specs=[SMEM]
        + [whole(ROWS, COLS)] * 4
        + [pl.BlockSpec((1, ROWS, COLS), lambda g: (g, 0, 0))]
        + [whole(N_ROWS, COLS), whole(S_ROWS, COLS), whole(3, FR, LANES), whole(FR, LANES)],
        out_specs=(
            whole(3, FR, FC),
            pl.BlockSpec((1, 5, FR, FC), lambda g: (g, 0, 0, 0)),
            pl.BlockSpec((1, 2 * LANES, FC), lambda g: (g, 0, 0)),
        ),
        scratch_shapes=[
            pltpu.VMEM((16 + ROWS + NHALO, COLS), F32),
            pltpu.VMEM((FR + 8, FC), F32),
            pltpu.VMEM((FR + 8, FC), F32),
            pltpu.VMEM((4, FR, LANES), F32),
        ],
        compiler_params=limits(48),
        cost_estimate=pl.CostEstimate(
            flops=60_000_000, bytes_accessed=27_000_000, transcendentals=0
        ),
        name="prepare",
    )(
        shifts, elevation, flux_x, flux_y, depth, wet_mask, from_north, from_south,
        from_east, from_west,
    )

    coarse, edge = pl.pallas_call(
        receive_kernel,
        out_shape=(sds((STEPS, COARSE, LANES), F32), sds((3, CAP, LANES), F32)),
        in_specs=[VMEM],
        out_specs=(VMEM, VMEM),
        compiler_params=limits(40),
        cost_estimate=pl.CostEstimate(flops=300_000_000, bytes_accessed=2_700_000, transcendentals=0),
        name="receive_rows",
    )(got)
    coarse_north = ring(coarse, "ny", -1)
    coarse_south = ring(coarse, "ny", 1)
    north_flag = lax.axis_index("ny") < lax.axis_size("ny") - 1
    tall = jnp.concatenate(
        [coarse_south[:, 8:], coarse, jnp.where(north_flag, coarse_north[:, :8], 0.0)], axis=1
    )
    tall_east = ring(tall, "nx", -1)
    tall_west = ring(tall, "nx", 1)

    step_tall = pl.BlockSpec((1, 32, LANES), lambda g: (g, 0, 0))
    return pl.pallas_call(
        steps_kernel,
        out_shape=(sds((ROWS, COLS), F32),) * 3,
        grid=(STEPS,),
        in_specs=[
            SMEM,
            whole(3, FR, FC),
            pl.BlockSpec((1, 5, FR, FC), lambda g: (g, 0, 0, 0)),
            pl.BlockSpec((1, 2 * LANES, FC), lambda g: (g, 0, 0)),
            step_tall,
            step_tall,
            step_tall,
            whole(3, CAP, LANES),
        ],
        out_specs=(whole(ROWS, COLS),) * 3,
        scratch_shapes=[
            pltpu.VMEM((3, FR + 16, FC), F32),
            pltpu.VMEM((FR, FC), F32),
            pltpu.VMEM((3, 16, FC), F32),
        ],
        compiler_params=limits(48),
        cost_estimate=pl.CostEstimate(
            flops=400_000_000, bytes_accessed=23_000_000, transcendentals=0
        ),
        name="steps",
    )(shifts, state, coef, cols, tall, tall_east, tall_west, edge)


def solution(mesh):
    in_specs = (
        P("ny", "nx"),
        P("ny", "nx"),
        P("ny", "nx"),
        P("ny", "nx"),
        P(None, "ny", "nx"),
        P(),
        P(None, ("ny", "nx"), None),
        P(None, ("ny", "nx")),
        P(None, ("ny", "nx")),
        P(None, "ny"),
        P(None, "nx", "ny"),
    )
    out_specs = (P("ny", "nx"), P("ny", "nx"), P("ny", "nx"))
    return jax.shard_map(local, mesh=mesh, in_specs=in_specs, out_specs=out_specs, check_vma=False)
```

profile of v0, /device:TPU:0, one launch (start us, length us, event | category | flops | bytes accessed | tf_op | source)
XLA Modules:
  0.0 122.5 jit_solution(7593105903444534797)
XLA Ops:
  5.8 1.9 %pack_rows.1 = f32[128,40,128]{2,1,0:T(8,128)S(1)} custom-call(s32[4,256]{1,0:T(4,128)S(1)} %copy-done.13, s32[256,4]{1,0:T(8,128)S(1)} %bitcast.25, s32[256,4]{1,0:T(8,128)S(1)} %bitcast.24, f32[4,256,128]{2,1,0:T(8,128)S(1)} %copy-done.12, f32[8,128]{1,0:T(8,128)S(1)} %pad.4.edge_ref), custom_call_target="tpu_custom_call" | custom-call | flops 800000000 | bytes 3200000 | tf_op jit(solution)/shard_map/pack_rows/pallas_call | solution.py:386
  7.7 1.6 %copy-done.1 = f32[128,40,128]{2,1,0:T(8,128)} copy-done((f32[128,40,128]{2,1,0:T(8,128)}, f32[128,40,128]{2,1,0:T(8,128)S(1)}, u32[]{:S(2)}) %copy-start.1) | copy-done | bytes 2621464
  9.3 11.6 %all-to-all-start = ((f32[128,40,128]{2,1,0:T(8,128)}), f32[128,40,128]{2,1,0:T(8,128)}, u32[]{:S(2)}, u32[]{:S(2)}) async-start(f32[128,40,128]{2,1,0:T(8,128)} %copy-done.1), calls=%async_computation | async-start | bytes 5242880 | tf_op jit(solution)/shard_map/all_to_all | solution.py:395
  22.2 1.4 %slice_dynamic-update-slice_fusion.6 = f32[64,1152]{1,0:T(8,128)} fusion(f32[64,1152]{1,0:T(8,128)} %slice_dynamic-update-slice_fusion.7, f32[144,1152]{1,0:T(8,128)} %u_ref.3), kind=kLoop, calls=%fused_computation.17 | loop fusion | bytes 73728
  23.6 1.4 %slice_dynamic-update-slice_fusion.5 = f32[64,1152]{1,0:T(8,128)} fusion(f32[64,1152]{1,0:T(8,128)} %slice_dynamic-update-slice_fusion.6, f32[144,1152]{1,0:T(8,128)} %v_ref.3), kind=kLoop, calls=%fused_computation.16 | loop fusion | bytes 73728
  25.0 1.4 %slice_dynamic-update-slice_fusion.4 = f32[64,1152]{1,0:T(8,128)} fusion(f32[64,1152]{1,0:T(8,128)} %slice_dynamic-update-slice_fusion.5, f32[144,1152]{1,0:T(8,128)} %b_ref.3), kind=kLoop, calls=%fused_computation.15 | loop fusion | bytes 73728
  27.6 1.6 %slice_dynamic-update-slice_fusion.1 = f32[232,1152]{1,0:T(8,128)} fusion(f32[232,1152]{1,0:T(8,128)} %slice_dynamic-update-slice_fusion.2, f32[144,1152]{1,0:T(8,128)} %u_ref.3), kind=kLoop, calls=%fused_computation.2 | loop fusion | bytes 368640
  29.2 1.6 %slice_dynamic-update-slice_fusion = f32[232,1152]{1,0:T(8,128)} fusion(f32[232,1152]{1,0:T(8,128)} %slice_dynamic-update-slice_fusion.1, f32[144,1152]{1,0:T(8,128)} %v_ref.3), kind=kLoop, calls=%fused_computation.1 | loop fusion | bytes 368640
  30.9 1.6 %slice_dynamic-update-slice_fusion.3 = f32[232,1152]{1,0:T(8,128)} fusion(f32[232,1152]{1,0:T(8,128)} %slice_dynamic-update-slice_fusion, f32[144,1152]{1,0:T(8,128)} %b_ref.3), kind=kLoop, calls=%fused_computation.5 | loop fusion | bytes 294912
  35.6 1.9 %collective-permute-start = (f32[232,1152]{1,0:T(8,128)}, f32[232,1152]{1,0:T(8,128)}, u32[]{:S(2)}, u32[]{:S(2)}) collective-permute-start(f32[232,1152]{1,0:T(8,128)} %get-tuple-element.14), channel_id=1, source_target_pairs={{0,112},{16,0},{32,16},{48,32},{64,48},{80,64},{96,80},{112,96},{1... | collective-permute-start | bytes 3207176 | tf_op jit(solution)/shard_map/ppermute | solution.py:358
  37.6 16.7 %collective-permute-done.1.south_ref = f32[64,1152]{1,0:T(8,128)} collective-permute-done((f32[64,1152]{1,0:T(8,128)}, f32[64,1152]{1,0:T(8,128)}, u32[]{:S(2)}, u32[]{:S(2)}) %collective-permute-start.1) | collective-permute-done | bytes 294944 | tf_op jit(solution)/shard_map/ppermute | solution.py:358
  54.3 5.0 %collective-permute-done.north_ref = f32[232,1152]{1,0:T(8,128)} collective-permute-done((f32[232,1152]{1,0:T(8,128)}, f32[232,1152]{1,0:T(8,128)}, u32[]{:S(2)}, u32[]{:S(2)}) %collective-permute-start) | collective-permute-done | bytes 1069088 | tf_op jit(solution)/shard_map/ppermute | solution.py:358
  59.3 1.1 copy-done.3
  62.5 2.1 %pack_sides.1 = f32[2,3,152,128]{3,2,1,0:T(8,128)S(1)} custom-call(s32[4,2]{1,0:T(4,128)S(1)} %copy.18.shifts_ref, f32[144,1152]{1,0:T(8,128)S(1)} %copy-done.2, f32[144,1152]{1,0:T(8,128)S(1)} %copy-done.3, f32[144,1152]{1,0:T(8,128)S(1)} %copy-done.5, f32[144,1152]{1,0:T(8,128)S(1)} %copy-done.7, s32[4,144,1152]{2,1,0:T(8,128)S(1)} %copy-done, ...), custom_call_target="tpu_custom_call" | custom-call | flops 8000000 | bytes 2500000 | tf_op jit(solution)/shard_map/pack_sides/pallas_call | solution.py:399
  65.4 3.1 %receive_rows.1 = (f32[4,16,128]{2,1,0:T(8,128)S(1)}, f32[3,8,128]{2,1,0:T(8,128)S(1)}) custom-call(f32[128,40,128]{2,1,0:T(8,128)} %all-to-all-done.got_ref), custom_call_target="tpu_custom_call" | custom-call | flops 300000000 | bytes 2700000 | tf_op jit(solution)/shard_map/receive_rows/pallas_call | solution.py:450
  68.6 3.1 %collective-permute-start.5 = (f32[4,16,128]{2,1,0:T(8,128)S(1)}, f32[4,16,128]{2,1,0:T(8,128)S(1)}, u32[]{:S(2)}, u32[]{:S(2)}) collective-permute-start(f32[4,16,128]{2,1,0:T(8,128)S(1)} %get-tuple-element.11), channel_id=1, source_target_pairs={{0,112},{16,0},{32,16},{48,32},{64,48},{80,64},{96,80},{112,96},{1... | collective-permute-start | bytes 98312 | tf_op jit(solution)/shard_map/ppermute | solution.py:358
  72.6 1.8 %collective-permute-start.3 = (f32[152,128]{1,0:T(8,128)S(1)}, f32[152,128]{1,0:T(8,128)S(1)}, u32[]{:S(2)}, u32[]{:S(2)}) collective-permute-start(f32[152,128]{1,0:T(8,128)S(1)} %slice_bitcast_fusion.1), channel_id=1, source_target_pairs={{0,1},{1,2},{2,3},{3,4},{4,5},{5,6},{6,7},{7,8},{8,9},{9,10},{10,1... | collective-permute-start | bytes 233480 | tf_op jit(solution)/shard_map/ppermute | solution.py:358
  74.4 4.1 %collective-permute-start.2 = (f32[3,152,128]{2,1,0:T(8,128)S(1)}, f32[3,152,128]{2,1,0:T(8,128)S(1)}, u32[]{:S(2)}, u32[]{:S(2)}) collective-permute-start(f32[3,152,128]{2,1,0:T(8,128)S(1)} %slice_bitcast_fusion), channel_id=1, source_target_pairs={{0,15},{1,0},{2,1},{3,2},{4,3},{5,4},{6,5},{7,6},{8,7},{9,8},{10,9... | collective-permute-start | bytes 700424 | tf_op jit(solution)/shard_map/ppermute | solution.py:358
  78.5 4.5 %collective-permute-done.4 = f32[4,16,128]{2,1,0:T(8,128)S(1)} collective-permute-done((f32[4,16,128]{2,1,0:T(8,128)S(1)}, f32[4,16,128]{2,1,0:T(8,128)S(1)}, u32[]{:S(2)}, u32[]{:S(2)}) %collective-permute-start.4) | collective-permute-done | bytes 32800 | tf_op jit(solution)/shard_map/ppermute | solution.py:358
  83.2 5.3 %collective-permute-start.6 = (f32[4,32,128]{2,1,0:T(8,128)S(1)}, f32[4,32,128]{2,1,0:T(8,128)S(1)}, u32[]{:S(2)}, u32[]{:S(2)}) collective-permute-start(f32[4,32,128]{2,1,0:T(8,128)S(1)} %pad_maximum_fusion.own_ref), channel_id=1, source_target_pairs={{0,15},{1,0},{2,1},{3,2},{4,3},{5,4},{6,5},{7,6},{8,7},{9,8},{10,9... | collective-permute-start | bytes 196616 | tf_op jit(solution)/shard_map/ppermute | solution.py:358
  88.5 12.8 %prepare.1 = (f32[3,152,1280]{2,1,0:T(8,128)}, f32[4,5,152,1280]{3,2,1,0:T(8,128)}, bf16[4,256,1280]{2,1,0:T(8,128)(2,1)}) custom-call(s32[4,2]{1,0:T(4,128)S(1)} %copy.18.shifts_ref, f32[144,1152]{1,0:T(8,128)S(1)} %copy-done.2, f32[144,1152]{1,0:T(8,128)S(1)} %copy-done.4, f32[144,1152]{1,0:T(8,128)S(1)} %copy-done.6, f32[144,1152]{1,0:T(8,128)S(1)} %copy-done.8, ...), custom_call_target="tpu_custom_call" | custom-call | flops 60000000 | bytes 27000000 | tf_op jit(solution)/shard_map/prepare/pallas_call | solution.py:417
  101.4 1.7 %copy-done.9 = bf16[4,256,1280]{2,1,0:T(8,128)(2,1)S(1)} copy-done((bf16[4,256,1280]{2,1,0:T(8,128)(2,1)S(1)}, bf16[4,256,1280]{2,1,0:T(8,128)(2,1)}, u32[]{:S(2)}) %copy-start.9) | copy-done | bytes 2621464
  103.1 1.7 %copy-done.10 = f32[3,152,1280]{2,1,0:T(8,128)S(1)} copy-done((f32[3,152,1280]{2,1,0:T(8,128)S(1)}, f32[3,152,1280]{2,1,0:T(8,128)}, u32[]{:S(2)}) %copy-start.10) | copy-done | bytes 2334744
  104.8 17.8 %steps.1 = (f32[144,1152]{1,0:T(8,128)}, f32[144,1152]{1,0:T(8,128)}, f32[144,1152]{1,0:T(8,128)}) custom-call(s32[4,2]{1,0:T(4,128)S(1)} %copy.18.shifts_ref, f32[3,152,1280]{2,1,0:T(8,128)S(1)} %copy-done.10, f32[4,5,152,1280]{3,2,1,0:T(8,128)} %get-tuple-element.9.coef_ref, bf16[4,256,1280]{2,1,0:T(8,128)(2,1)S(1)} %copy-done.9, ...), custom_call_target="tpu_custom_call" | custom-call | flops 400000000 | bytes 23000000 | tf_op jit(solution)/shard_map/steps/pallas_call | solution.py:469
  (59 shorter events, 15.0 us)
Async XLA Ops:
  4.0 1.0 copy-start.12
  5.1 0.7 copy-start.13
  7.7 1.6 %copy-start.1 = (f32[128,40,128]{2,1,0:T(8,128)}, f32[128,40,128]{2,1,0:T(8,128)S(1)}, u32[]{:S(2)}) copy-start(f32[128,40,128]{2,1,0:T(8,128)S(1)} %pack_rows.1) | copy-start | bytes 7864324
  9.3 11.6 %copy-start.2 = (f32[144,1152]{1,0:T(8,128)S(1)}, f32[144,1152]{1,0:T(8,128)}, u32[]{:S(2)}) copy-start(f32[144,1152]{1,0:T(8,128)} %e_ref.3) | copy-start | bytes 1990660
  9.3 17.1 %copy-start = (s32[4,144,1152]{2,1,0:T(8,128)S(1)}, s32[4,144,1152]{2,1,0:T(8,128)}, u32[]{:S(2)}) copy-start(s32[4,144,1152]{2,1,0:T(8,128)} %m_ref.3) | copy-start | bytes 7962628
  9.3 56.1 %all-to-all-start = ((f32[128,40,128]{2,1,0:T(8,128)}), f32[128,40,128]{2,1,0:T(8,128)}, u32[]{:S(2)}, u32[]{:S(2)}) async-start(f32[128,40,128]{2,1,0:T(8,128)} %copy-done.1), calls=%async_computation | async-start | bytes 5242880 | tf_op jit(solution)/shard_map/all_to_all | solution.py:395
  25.0 12.5 %copy-start.14 = (s32[4,2]{0,1:T(2,128)S(1)}, s32[4,2]{0,1:T(2,128)}, u32[]{:S(2)}) copy-start(s32[4,2]{0,1:T(2,128)} %param.16) | copy-start | bytes 100
  35.6 23.6 %collective-permute-start = (f32[232,1152]{1,0:T(8,128)}, f32[232,1152]{1,0:T(8,128)}, u32[]{:S(2)}, u32[]{:S(2)}) collective-permute-start(f32[232,1152]{1,0:T(8,128)} %get-tuple-element.14), channel_id=1, source_target_pairs={{0,112},{16,0},{32,16},{48,32},{64,48},{80,64},{96,80},{112,96},{1... | collective-permute-start | bytes 3207176 | tf_op jit(solution)/shard_map/ppermute | solution.py:358
  37.5 16.8 %collective-permute-start.1 = (f32[64,1152]{1,0:T(8,128)}, f32[64,1152]{1,0:T(8,128)}, u32[]{:S(2)}, u32[]{:S(2)}) collective-permute-start(f32[64,1152]{1,0:T(8,128)} %get-tuple-element.13), channel_id=1, source_target_pairs={{0,16},{16,32},{32,48},{48,64},{64,80},{80,96},{96,112},{112,0},{1... | collective-permute-start | bytes 884744 | tf_op jit(solution)/shard_map/ppermute | solution.py:358
  59.3 1.1 copy-start.3
  60.3 1.1 copy-start.5
  61.4 1.1 copy-start.7
  64.6 0.8 copy-start.11
  65.4 23.1 %copy-start.4 = (f32[144,1152]{1,0:T(8,128)S(1)}, f32[144,1152]{1,0:T(8,128)}, u32[]{:S(2)}) copy-start(f32[144,1152]{1,0:T(8,128)} %u_ref.3) | copy-start | bytes 1990660
  65.4 23.1 %copy-start.6 = (f32[144,1152]{1,0:T(8,128)S(1)}, f32[144,1152]{1,0:T(8,128)}, u32[]{:S(2)}) copy-start(f32[144,1152]{1,0:T(8,128)} %v_ref.3) | copy-start | bytes 1990660
  65.4 23.1 %copy-start.8 = (f32[144,1152]{1,0:T(8,128)S(1)}, f32[144,1152]{1,0:T(8,128)}, u32[]{:S(2)}) copy-start(f32[144,1152]{1,0:T(8,128)} %b_ref.3) | copy-start | bytes 1990660
  68.6 10.0 %collective-permute-start.5 = (f32[4,16,128]{2,1,0:T(8,128)S(1)}, f32[4,16,128]{2,1,0:T(8,128)S(1)}, u32[]{:S(2)}, u32[]{:S(2)}) collective-permute-start(f32[4,16,128]{2,1,0:T(8,128)S(1)} %get-tuple-element.11), channel_id=1, source_target_pairs={{0,112},{16,0},{32,16},{48,32},{64,48},{80,64},{96,80},{112,96},{1... | collective-permute-start | bytes 98312 | tf_op jit(solution)/shard_map/ppermute | solution.py:358
  72.6 15.9 %collective-permute-start.3 = (f32[152,128]{1,0:T(8,128)S(1)}, f32[152,128]{1,0:T(8,128)S(1)}, u32[]{:S(2)}, u32[]{:S(2)}) collective-permute-start(f32[152,128]{1,0:T(8,128)S(1)} %slice_bitcast_fusion.1), channel_id=1, source_target_pairs={{0,1},{1,2},{2,3},{3,4},{4,5},{5,6},{6,7},{7,8},{8,9},{9,10},{10,1... | collective-permute-start | bytes 233480 | tf_op jit(solution)/shard_map/ppermute | solution.py:358
  74.4 14.1 %collective-permute-start.2 = (f32[3,152,128]{2,1,0:T(8,128)S(1)}, f32[3,152,128]{2,1,0:T(8,128)S(1)}, u32[]{:S(2)}, u32[]{:S(2)}) collective-permute-start(f32[3,152,128]{2,1,0:T(8,128)S(1)} %slice_bitcast_fusion), channel_id=1, source_target_pairs={{0,15},{1,0},{2,1},{3,2},{4,3},{5,4},{6,5},{7,6},{8,7},{9,8},{10,9... | collective-permute-start | bytes 700424 | tf_op jit(solution)/shard_map/ppermute | solution.py:358
  78.5 4.6 %collective-permute-start.4 = (f32[4,16,128]{2,1,0:T(8,128)S(1)}, f32[4,16,128]{2,1,0:T(8,128)S(1)}, u32[]{:S(2)}, u32[]{:S(2)}) collective-permute-start(f32[4,16,128]{2,1,0:T(8,128)S(1)} %get-tuple-element.11), channel_id=1, source_target_pairs={{0,16},{16,32},{32,48},{48,64},{64,80},{80,96},{96,112},{112,0},{1... | collective-permute-start | bytes 98312 | tf_op jit(solution)/shard_map/ppermute | solution.py:358
  83.1 18.2 %collective-permute-start.7 = (f32[4,32,128]{2,1,0:T(8,128)S(1)}, f32[4,32,128]{2,1,0:T(8,128)S(1)}, u32[]{:S(2)}, u32[]{:S(2)}) collective-permute-start(f32[4,32,128]{2,1,0:T(8,128)S(1)} %pad_maximum_fusion.own_ref), channel_id=1, source_target_pairs={{0,1},{1,2},{2,3},{3,4},{4,5},{5,6},{6,7},{7,8},{8,9},{9,10},{10,1... | collective-permute-start | bytes 196616 | tf_op jit(solution)/shard_map/ppermute | solution.py:358
  83.2 18.2 %collective-permute-start.6 = (f32[4,32,128]{2,1,0:T(8,128)S(1)}, f32[4,32,128]{2,1,0:T(8,128)S(1)}, u32[]{:S(2)}, u32[]{:S(2)}) collective-permute-start(f32[4,32,128]{2,1,0:T(8,128)S(1)} %pad_maximum_fusion.own_ref), channel_id=1, source_target_pairs={{0,15},{1,0},{2,1},{3,2},{4,3},{5,4},{6,5},{7,6},{8,7},{9,8},{10,9... | collective-permute-start | bytes 196616 | tf_op jit(solution)/shard_map/ppermute | solution.py:358
  101.4 1.7 %copy-start.9 = (bf16[4,256,1280]{2,1,0:T(8,128)(2,1)S(1)}, bf16[4,256,1280]{2,1,0:T(8,128)(2,1)}, u32[]{:S(2)}) copy-start(bf16[4,256,1280]{2,1,0:T(8,128)(2,1)} %get-tuple-element.10.cols_ref) | copy-start | bytes 7864324
  103.1 1.7 %copy-start.10 = (f32[3,152,1280]{2,1,0:T(8,128)S(1)}, f32[3,152,1280]{2,1,0:T(8,128)}, u32[]{:S(2)}) copy-start(f32[3,152,1280]{2,1,0:T(8,128)} %get-tuple-element.8.state_ref) | copy-start | bytes 7004164
where the time goes:
time: 123 us
  Pallas kernels  37.7 us (31%)
  starting transfers between devices  27.9 us (23%)
  waiting for transfers between devices  26.2 us (21%)
  local copies, waits for them, and re-layouts  24 us (20%)
  other arithmetic  5.9 us (5%)
    ppermute x8, waiting for transfers between devices, ring(): lax.ppermute(value, axis, [(i, (i + by) % count) for i in range(count)])  26.2 us
    unnamed x41, local copies, waits for them, and re-layouts  22.7 us
    pallas_call x1, Pallas kernels, local(): pl.pallas_call(steps_kernel, out_shape=(sds((ROWS, COLS), F32),) * 3, gri...  17.8 us
    ppermute x8, starting transfers between devices, ring(): lax.ppermute(value, axis, [(i, (i + by) % count) for i in range(count)])  16.3 us
    pallas_call x1, Pallas kernels, local(): pl.pallas_call(prepare_kernel, out_shape=(sds((3, FR, FC), F32), sds((STE...  12.8 us
    all_to_all x1, starting transfers between devices, local(): lax.all_to_all(send, ('ny', 'nx'), split_axis=0, concat_axis=0, tiled=True)  11.6 us
    unnamed x7, other arithmetic  4.52 us
    pallas_call x1, Pallas kernels, local(): pl.pallas_call(receive_kernel, out_shape=(sds((STEPS, COARSE, LANES), F32...  3.15 us
  transfers between devices with their start and end apart: 9, of which 3 were waited for; matrix products, arithmetic and copies ran while one was open for 13% of the time, Pallas kernels for 12%

commit v1 on v0

v1 whole, which is shorter than its diff:
```python
import functools

import jax
import jax.numpy as jnp
from jax import lax
from jax.experimental import pallas as pl
from jax.experimental.pallas import tpu as pltpu
from jax.sharding import PartitionSpec as P

RATIO = 9
STEPS = 4
CAP = 8
COARSE = 16
LANES = 128
ROWS, COLS = 144, 1152
FR, FC = 152, 1280
ROW0, COL0 = 4, 40
NHALO = 40
WIDTHS = (32, 24, 16, 8)
N_E, N_B, N_M = 0, 120, (152, 184, 208, 224)
N_ROWS, S_ROWS = 232, 64
CHUNK = 40
PREPARE_MIB, STEPS_MIB = 63, 63
META = 124
KTILE, FTILE = COLS // LANES, FC // LANES
E_PLACE = ((0, 0), (0, 40), (0, 80), (1, 0), (1, 64), (2, 0), (2, 32), (1, 32), (1, 88), (2, 16), (2, 40))
E_WIDTH = (40, 40, 40, 32, 24, 16, 8, 32, 24, 16, 8)

F32, BF16, I32 = jnp.float32, jnp.bfloat16, jnp.int32
VMEM = pl.BlockSpec(memory_space=pltpu.VMEM)
SMEM = pl.BlockSpec(memory_space=pltpu.SMEM)


def iota(shape, dim):
    return lax.broadcasted_iota(I32, shape, dim)


def left_over(shifts_ref, step, dim):
    total = jnp.int32(0)
    for later in range(STEPS):
        total += jnp.where(later > step, shifts_ref[dim, later], 0)
    return total


def halves(x):
    high = x.astype(BF16)
    return high, (x - high.astype(F32)).astype(BF16)


def dot(a, b, dims=((1,), (0,))):
    return lax.dot_general(a, b, (dims, ((), ())), preferred_element_type=F32)


def message_kernel(
    e_top, u_top, v_top, b_top, m_top, e_low, u_low, v_low, b_low, m_low, north_ref, south_ref
):
    for f, ref in enumerate((e_top, u_top, v_top)):
        north_ref[N_E + NHALO * f : N_E + NHALO * (f + 1), :] = ref[...]
    north_ref[N_B : N_B + WIDTHS[0], :] = b_top[...]
    for f, ref in enumerate((e_low, u_low, v_low, b_low)):
        south_ref[8 * f : 8 * f + 8, :] = ref[...]
    for s in range(STEPS):
        north_ref[N_M[s] : N_M[s] + WIDTHS[s], :] = m_top[s, : WIDTHS[s], :].astype(F32)
        south_ref[32 + 8 * s : 40 + 8 * s, :] = m_low[s].astype(F32)


def pack_kernel(owner_ref, dest_ref, coarse_ref, vals_ref, panel_ref, after_ref, out_ref):
    del after_ref
    owners = out_ref.shape[0]
    count = dest_ref.shape[1]
    before = iota((count, count), 0) < iota((count, count), 1)
    unit = jnp.where(iota((count, count), 0) == iota((count, count), 1), 1.0, 0.0).astype(BF16)
    numbers = jnp.concatenate([dest_ref[...], coarse_ref[...] + 1], axis=0).astype(F32)
    upright = dot(unit, numbers.astype(BF16), ((1,), (1,)))
    lane = iota((count, LANES), 1)
    place_row = iota((owners * CAP, count), 0)
    meta = jnp.zeros((owners * CAP, LANES), F32)
    for s in range(STEPS):
        dest = dest_ref[s : s + 1, :]
        same = (upright[:, s : s + 1] == dest.astype(F32)) & before
        slot = jnp.sum(jnp.where(same, 1.0, 0.0), axis=0, keepdims=True).astype(I32)
        hits = jnp.where(place_row == dest * CAP + slot, 1.0, 0.0).astype(BF16)
        high, low = halves(vals_ref[s])
        target = jnp.where(lane == META + s, upright[:, STEPS + s : STEPS + s + 1], 0.0)
        out_ref[:, s * CAP : (s + 1) * CAP, :] = (dot(hits, high) + dot(hits, low)).reshape(
            owners, CAP, LANES
        )
        meta += dot(hits, target.astype(BF16))
    lane1 = iota((1, LANES), 1)
    first, second = [], []
    for s in range(STEPS):
        mine = owner_ref[0:1, s : s + 1] == lax.axis_index("nx")
        head = panel_ref[s, :, 0:LANES]
        tail = jnp.concatenate(
            [panel_ref[s, :, LANES:ROWS], jnp.zeros((1, 2 * LANES - ROWS), F32)], axis=1
        )
        first.append(jnp.where((lane1 < 120) & mine, head, 0.0))
        both = jnp.where(lane1 < 8, pltpu.roll(head, 8, 1), pltpu.roll(tail, 8, 1))
        second.append(jnp.where((lane1 < 24) & mine, both, 0.0))
    edges = jnp.concatenate(first + second, axis=0)
    out_ref[:, STEPS * CAP :, :] = meta.reshape(owners, CAP, LANES) + edges[None]


def receive_kernel(got_ref, after_ref, coarse_ref, edge_ref):
    del after_ref
    sources = got_ref.shape[0]
    meta = got_ref[:, STEPS * CAP :, :].reshape(sources * CAP, LANES)
    choose = jnp.where(iota((8, LANES), 1) == META + iota((8, LANES), 0), 1.0, 0.0)
    targets = dot(choose.astype(BF16), meta.astype(BF16), ((1,), (1,)))
    index = iota((COARSE, sources * CAP), 0)
    for s in range(STEPS):
        hits = jnp.where(index == targets[s : s + 1, :].astype(I32) - 1, 1.0, 0.0).astype(BF16)
        high, low = halves(got_ref[:, s * CAP : (s + 1) * CAP, :].reshape(sources * CAP, LANES))
        coarse_ref[s] = dot(hits, high) + dot(hits, low)
    row_block, col_groups = lax.axis_index("ny"), lax.axis_size("nx")
    for k in range(3):
        block = jnp.clip(row_block + k - 1, 0, lax.axis_size("ny") - 1)
        edge_ref[k] = jnp.sum(
            got_ref[pl.ds(block * col_groups, col_groups), STEPS * CAP :, :], axis=0
        )


def edge_flags():
    row_block, col_block = lax.axis_index("ny"), lax.axis_index("nx")
    south = jnp.where(row_block == 0, 0.0, 1.0).astype(F32)
    north = jnp.where(row_block == lax.axis_size("ny") - 1, 0.0, 1.0).astype(F32)
    west = jnp.where(col_block == 0, 0.0, 1.0).astype(F32)
    east = jnp.where(col_block == lax.axis_size("nx") - 1, 0.0, 1.0).astype(F32)
    return south, north, west, east


def fill_rows(tall_ref, own, south_ref, field, north_ref, north_at, width, flags):
    south, north = flags[0], flags[1]
    for k in range(tall_ref.shape[0]):
        lanes = slice(k * LANES, (k + 1) * LANES)
        tall_ref[k, 0:8, :] = south_ref[8 * field : 8 * field + 8, lanes] * south
        tall_ref[k, 8 : 8 + ROWS, :] = own(lanes)
        tall_ref[k, 8 + ROWS : 8 + ROWS + width, :] = (
            north_ref[north_at : north_at + width, lanes] * north
        )


def side_tiles(east_ref, west_ref, which, flags):
    tile, at = E_PLACE[which]
    right = east_ref[tile]
    if at:
        right = pltpu.roll(right, LANES - at, 1)
    left = pltpu.roll(west_ref[...], 120 - 8 * which, 1)
    return left * flags[2], right * flags[3]


def framed(ext, row_shift, col_shift, strips, write):
    lane = iota((FR, LANES), 1)
    turn = 128 - COL0 + col_shift
    amount = LANES - turn
    keep = lane < amount
    done, this = None, None
    for k in strips:
        if done != k:
            this = pltpu.roll(ext(k), amount, 1)
        following = pltpu.roll(ext(k + 1), amount, 1)
        write(k, jnp.where(keep, this, following))
        done, this = k + 1, following


def to_east(x, following, last_lane):
    return jnp.where(
        last_lane, pltpu.roll(following, LANES - 1, 1), pltpu.roll(x, LANES - 1, 1)
    )


def divide_18(n):
    return (n * 3641) >> 16


def frame_fields(
    shifts_ref, load, left_of, right_of, wet_ref, deep_ref,
    strips, state_to, coef_to, coef_strips, aside,
):
    def ext(which, tile_rows, row_shift):
        rows = pl.ds(row_shift + ROW0, FR)

        def tile(k):
            if k == 0:
                return left_of(which)
            if k == KTILE + 1:
                return right_of(which)
            return tile_rows(k - 1, rows)

        return tile

    row_all, col_all = left_over(shifts_ref, -1, 0), left_over(shifts_ref, -1, 1)
    for f in range(3):
        tiles = ext(f, load(f), row_all)
        aside(f, tiles)
        framed(tiles, row_all, col_all, coef_strips, functools.partial(state_to, f))
    wet_ref[:, FR:, :] = jnp.zeros_like(wet_ref[:, FR:, :])
    deep_ref[:, FR:, :] = jnp.zeros_like(deep_ref[:, FR:, :])
    last_lane = iota((8, LANES), 1) == LANES - 1
    row, lane = iota((FR, LANES), 0), iota((FR, LANES), 1)
    is_west = lax.axis_index("nx") == 0
    tile_rows = load(3)
    for s in range(STEPS):
        row_left, col_left = left_over(shifts_ref, s, 0), left_over(shifts_ref, s, 1)

        def write_depth(k, x, s=s):
            deep_ref[s * FTILE + k, 0:FR, :] = x

        tiles = ext(3 + s, tile_rows, row_left)
        aside(3 + s, tiles)
        framed(tiles, row_left, col_left, strips, write_depth)
    for s in range(STEPS):
        row_left, col_left = left_over(shifts_ref, s, 0), left_over(shifts_ref, s, 1)
        tiles = ext(7 + s, load(4 + s), row_left)
        aside(7 + s, tiles)
        nest_row = lax.axis_index("ny") * ROWS + row + row_left - ROW0
        in_nest = (nest_row >= 0) & (nest_row < ROWS * lax.axis_size("ny"))
        ghost = in_nest & (lane == COL0 - 1 - col_left) & is_west

        def write_wet(k, x, s=s, ghost=ghost):
            if k in coef_strips:
                coef_to(s, 4, k, slice(0, FR), x)
            wet_ref[k, 0:FR, :] = jnp.where(ghost, 1.0, x) if k == 0 else x

        framed(tiles, row_left, col_left, strips, write_wet)
        for k in coef_strips:
            east = min(k + 1, FTILE - 1)
            for at in range(0, FR, 8):
                tile, above = slice(at, at + 8), slice(at + 1, at + 9)
                wet, deep = wet_ref[k, tile, :], deep_ref[s * FTILE + k, tile, :]
                wet_e = to_east(wet, wet_ref[east, tile, :], last_lane)
                deep_e = to_east(deep, deep_ref[s * FTILE + east, tile, :], last_lane)
                wet = 0.0625 * wet
                open_x = wet * wet_e
                open_y = wet * wet_ref[k, above, :]
                coef_to(s, 0, k, tile, open_x)
                coef_to(s, 1, k, tile, open_x * (deep + deep_e))
                coef_to(s, 2, k, tile, open_y)
                coef_to(s, 3, k, tile, open_y * (deep + deep_ref[s * FTILE + k, above, :]))


def prepare_kernel(
    shifts_ref, e_ref, u_ref, v_ref, b_ref, m_ref, north_ref, south_ref,
    state_ref, coef_ref, cols_ref, ends_ref, east_ref, west_ref, tall_ref, wet_ref, deep_ref,
):
    flags = edge_flags()
    own_of = [lambda lanes, ref=ref: ref[:, lanes] for ref in (e_ref, u_ref, v_ref, b_ref)]
    own_of += [lambda lanes, s=s: m_ref[s, :, lanes].astype(F32) for s in range(STEPS)]
    starts = (N_E, N_E + NHALO, N_E + 2 * NHALO, N_B, *N_M)
    widths = (NHALO,) * 3 + (WIDTHS[0],) + WIDTHS
    lane = iota((FR, LANES), 1)
    tall_ref[...] = jnp.zeros_like(tall_ref)
    east_ref[...] = jnp.zeros_like(east_ref)
    west_ref[...] = jnp.zeros_like(west_ref)

    def load(field):
        fill_rows(
            tall_ref, own_of[field], south_ref, field, north_ref, starts[field], widths[field], flags
        )
        for place, k in enumerate((0, 1, KTILE - 1)):
            ends_ref[field, place] = tall_ref[k]
        return lambda k, rows: tall_ref[k, rows, :]

    def aside(which, tiles):
        (tile, at), width = E_PLACE[which], E_WIDTH[which]
        moved = pltpu.roll(tiles(1), at, 1) if at else tiles(1)
        east_ref[tile] = jnp.where((lane >= at) & (lane < at + width), moved, east_ref[tile])
        at = 8 * which
        moved = pltpu.roll(tiles(KTILE), at + 8, 1)
        west_ref[...] = jnp.where((lane >= at) & (lane < at + 8), moved, west_ref[...])

    def none(which):
        return jnp.zeros((FR, LANES), F32)

    def state_to(f, k, x):
        state_ref[f, k - 1] = x

    def coef_to(s, c, k, rows, x):
        coef_ref[s, c, k - 1, rows, :] = x

    frame_fields(
        shifts_ref, load, none, none, wet_ref, deep_ref,
        range(1, FTILE), state_to, coef_to, range(1, FTILE - 1), aside,
    )
    for s in range(STEPS):
        col = iota((1, FC), 1) + left_over(shifts_ref, s, 1) - COL0
        inside = jnp.where(col < 0, col + COLS, jnp.where(col >= COLS, col - COLS, col))
        numerator = 2 * inside + 1 - RATIO
        lower = jnp.clip(divide_18(numerator + 18) - 1, 0, LANES - 2)
        weight = jnp.clip(numerator - 18 * lower, 0, 18)
        first = lower + jnp.where((col < 0) | (col >= COLS), LANES, 0)
        for part in range(2):
            place = iota((LANES, FC), 0) + part * LANES
            cols_ref[s, part * LANES : (part + 1) * LANES, :] = jnp.where(
                place == first, 18 - weight, jnp.where(place == first + 1, weight, 0)
            ).astype(F32).astype(BF16)


def side_strips_kernel(
    shifts_ref, ends_ref, east_ref, west_ref, after_ref, state_ref, coef_ref, wet_ref, deep_ref
):
    del after_ref
    flags = edge_flags()

    def load(field):
        return lambda k, rows: ends_ref[field, min(k, 2), rows, :]

    def state_to(f, k, x):
        state_ref[f, 1 if k else 0] = x

    def coef_to(s, c, k, rows, x):
        coef_ref[s, c, 1 if k else 0, rows, :] = x

    frame_fields(
        shifts_ref,
        load,
        lambda which: side_tiles(east_ref, west_ref, which, flags)[0],
        lambda which: side_tiles(east_ref, west_ref, which, flags)[1],
        wet_ref,
        deep_ref,
        (0, 1, FTILE - 1),
        state_to,
        coef_to,
        (0, FTILE - 1),
        lambda which, tiles: None,
    )


def one_step(
    s, shifts_ref, mid_ref, side_ref, cols_ref, own_ref, east_ref, west_ref, edge_ref, cur, new
):
    row_left, col_left = left_over(shifts_ref, s, 0), left_over(shifts_ref, s, 1)
    is_west = lax.axis_index("nx") == 0
    east = jnp.where(lax.axis_index("nx") == lax.axis_size("nx") - 1, 0.0, 1.0).astype(F32)

    i = iota((FR, 1), 0) + row_left - ROW0
    block = jnp.where(i < 0, 0, jnp.where(i >= ROWS, 2, 1))
    inside = i - (block - 1) * ROWS
    numerator = 2 * inside + 1 - RATIO
    lower = jnp.clip(divide_18(numerator + 18) - 1, 0, COARSE - 2)
    weight = jnp.clip(numerator - 18 * lower, 0, 18)
    first = lower + 16 * block - 8
    place = iota((FR, 32), 1)
    rows = jnp.where(place == first, 18 - weight, jnp.where(place == first + 1, weight, 0))
    rows = rows.astype(F32).astype(BF16)
    side = jnp.where(iota((32, LANES), 1) < 64, east_ref[s] * east, west_ref[s])
    parts = []
    for x in (own_ref[s], side):
        high, low = halves(x)
        parts.append(dot(rows, high) + dot(rows, low))
    section = jnp.concatenate(parts, axis=1) * (1.0 / 324.0)
    high, low = halves(section)
    for k in range(0, FTILE, 2):
        lanes = slice(k * LANES, (k + 2) * LANES)
        rise = dot(high, cols_ref[s, :, lanes]) + dot(low, cols_ref[s, :, lanes])
        cur[0, k, 0:FR, :] += rise[:, :LANES]
        cur[0, k + 1, 0:FR, :] += rise[:, LANES:]

    half = jnp.where(inside >= 120, 1, 0)
    pick = jnp.where(iota((FR, 24), 1) == 8 * block + 4 * half + s, 1.0, 0.0).astype(BF16)
    high, low = halves(edge_ref[...].reshape(24, LANES))
    line = dot(pick, high) + dot(pick, low)
    lane = iota((FR, LANES), 1)
    edge = jnp.sum(jnp.where(lane == inside - 120 * half, line, 0.0), axis=1, keepdims=True)
    ghost = (lane == COL0 - 1 - col_left) & is_west

    cur[0, 0, 0:FR, :] = jnp.where(ghost, edge, cur[0, 0, 0:FR, :])
    cur[1, 0, 0:FR, :] = jnp.where(ghost, 0.0, cur[1, 0, 0:FR, :])
    cur[2, 0, 0:FR, :] = jnp.where(ghost, 0.0, cur[2, 0, 0:FR, :])
    def cat(f, rows):
        return jnp.concatenate([cur[f, k, rows, :] for k in range(FTILE)], axis=1)

    def coefficient(c, rows):
        tiles = [mid_ref[s, c, k, rows, :] for k in range(FTILE - 2)]
        ends = [side_ref[s, c, k, rows, :] for k in range(2)]
        return jnp.concatenate([ends[0], *tiles, ends[1]], axis=1)

    first_row = iota((8, FC), 0) == 0
    south = [jnp.zeros((8, FC), F32)] * 3
    for at in range(0, FR, 8):
        tile, above = slice(at, at + 8), slice(at + 1, at + 9)
        E, U, V = (cat(f, tile) for f in range(3))
        Ee, Ue, Ve = (pltpu.roll(x, FC - 1, 1) for x in (E, U, V))
        bx, cx, by, cy, inner = (coefficient(c, tile) for c in range(5))
        across = (
            bx * (2.0 * (U + Ue) - (Ee - E)),
            cx * (E + Ee) - bx * (Ue - U),
            bx * (V - Ve),
        )
        out = [x - (a - pltpu.roll(a, 1, 1)) for x, a in zip((E, U, V), across)]
        En, Un, Vn = (cat(f, above) for f in range(3))
        along = (
            by * (2.0 * (V + Vn) - (En - E)),
            by * (U - Un),
            cy * (E + En) - by * (Vn - V),
        )
        for f in range(3):
            lifted = pltpu.roll(along[f], 1, 0)
            out[f] = out[f] - (along[f] - jnp.where(first_row, south[f], lifted))
            south[f] = lifted
        out = (out[0], inner * out[1], inner * out[2])
        for f in range(3):
            for k in range(FTILE):
                new[f, k, tile, :] = out[f][:, k * LANES : (k + 1) * LANES]


def steps_kernel(
    shifts_ref, mid_state, side_state, mid_hbm, side_hbm, cols_hbm, own_ref, east_ref, west_ref,
    edge_ref, e_out, u_out, v_out, even, odd, mid_ref, side_ref, cols_ref, sems,
):
    copies = []
    for f in range(3):
        copies.append(
            pltpu.make_async_copy(
                mid_state.at[f], even.at[f, 1 : FTILE - 1, 0:FR, :], sems.at[f]
            )
        )
        for end, k in enumerate((0, FTILE - 1)):
            copies.append(
                pltpu.make_async_copy(
                    side_state.at[f, end], even.at[f, k, 0:FR, :], sems.at[3 + 2 * f + end]
                )
            )
    per_step = []
    for s in range(STEPS):
        pairs = ((cols_hbm, cols_ref), (mid_hbm, mid_ref), (side_hbm, side_ref))
        per_step.append(
            [
                pltpu.make_async_copy(a.at[s], b.at[s], sems.at[9 + 3 * s + i])
                for i, (a, b) in enumerate(pairs)
            ]
        )
    for copy in copies:
        copy.start()
    for each in per_step:
        for copy in each:
            copy.start()
    for f in range(3):
        for k in range(FTILE):
            even[f, k, FR:, :] = jnp.zeros((8, LANES), F32)
            odd[f, k, FR:, :] = jnp.zeros((8, LANES), F32)
    for copy in copies:
        copy.wait()
    cur, new = even, odd
    for s in range(STEPS):
        for copy in per_step[s]:
            copy.wait()
        one_step(
            s, shifts_ref, mid_ref, side_ref, cols_ref, own_ref, east_ref, west_ref, edge_ref,
            cur, new,
        )
        cur, new = new, cur
    keep = iota((ROWS, LANES), 1) < LANES - COL0
    rows = slice(ROW0, ROW0 + ROWS)
    for f, ref in enumerate((e_out, u_out, v_out)):
        this = pltpu.roll(cur[f, 0, rows, :], LANES - COL0, 1)
        for k in range(KTILE):
            following = pltpu.roll(cur[f, k + 1, rows, :], LANES - COL0, 1)
            ref[:, k * LANES : (k + 1) * LANES] = jnp.where(keep, this, following)
            this = following


def ring(value, axis, by):
    count = lax.axis_size(axis)
    return lax.ppermute(value, axis, [(i, (i + by) % count) for i in range(count)])


def limits(mib, **more):
    return pltpu.CompilerParams(vmem_limit_bytes=mib * 1024 * 1024, **more)


def local(
    elevation, flux_x, flux_y, depth, wet_mask, shifts, parent_vals, row_dest, row_coarse,
    edge_owner, edge_panels,
):
    shifts = shifts.T
    owners = lax.axis_size("ny") * lax.axis_size("nx")
    sds = jax.ShapeDtypeStruct
    top = lambda rows: pl.BlockSpec((rows, COLS), lambda g: (0, 0))
    low = pl.BlockSpec((8, COLS), lambda g: (ROWS // 8 - 1, 0))
    fields = (elevation, flux_x, flux_y, depth, wet_mask)
    north_message, south_message = pl.pallas_call(
        message_kernel,
        out_shape=(sds((N_ROWS, COLS), F32), sds((S_ROWS, COLS), F32)),
        grid=(1,),
        in_specs=[top(NHALO)] * 3
        + [top(WIDTHS[0]), pl.BlockSpec((STEPS, WIDTHS[0], COLS), lambda g: (0, 0, 0))]
        + [low] * 4
        + [pl.BlockSpec((STEPS, 8, COLS), lambda g: (0, ROWS // 8 - 1, 0))],
        out_specs=(top(N_ROWS), top(S_ROWS)),
        compiler_params=limits(63),
        cost_estimate=pl.CostEstimate(flops=300_000, bytes_accessed=2_700_000, transcendentals=0),
        name="messages",
    )(*fields, *fields)
    from_north = ring(north_message, "ny", -1)
    from_south = ring(south_message, "ny", 1)

    send = pl.pallas_call(
        pack_kernel,
        out_shape=sds((owners, CHUNK, LANES), F32),
        in_specs=[VMEM] * 5 + [pl.BlockSpec(memory_space=pl.ANY)],
        out_specs=VMEM,
        compiler_params=limits(63),
        cost_estimate=pl.CostEstimate(flops=800_000_000, bytes_accessed=3_200_000, transcendentals=0),
        name="pack_rows",
    )(edge_owner.reshape(1, STEPS), row_dest, row_coarse, parent_vals, edge_panels, south_message)
    send, from_south, from_north = lax.optimization_barrier((send, from_south, from_north))
    got = lax.all_to_all(send, ("ny", "nx"), split_axis=0, concat_axis=0, tiled=True)

    frame = lambda *lead: sds((*lead, FR, LANES), F32)
    tall_rows = 16 + ROWS + NHALO
    mid_state, mid_coef, cols, ends, east_side, west_side = pl.pallas_call(
        prepare_kernel,
        out_shape=(
            frame(3, FTILE - 2),
            frame(STEPS, 5, FTILE - 2),
            sds((STEPS, 2 * LANES, FC), BF16),
            sds((4 + STEPS, 3, tall_rows, LANES), F32),
            frame(3),
            frame(),
        ),
        in_specs=[SMEM] + [VMEM] * 7,
        out_specs=(VMEM,) * 6,
        scratch_shapes=[
            pltpu.VMEM((KTILE, tall_rows, LANES), F32),
            pltpu.VMEM((FTILE, FR + 8, LANES), F32),
            pltpu.VMEM((STEPS * FTILE, FR + 8, LANES), F32),
        ],
        compiler_params=limits(PREPARE_MIB),
        cost_estimate=pl.CostEstimate(
            flops=60_000_000, bytes_accessed=27_000_000, transcendentals=0
        ),
        name="prepare",
    )(shifts, *fields, from_north, from_south)
    from_east = ring(east_side, "nx", -1)
    from_west = ring(west_side, "nx", 1)

    coarse, edge = pl.pallas_call(
        receive_kernel,
        out_shape=(sds((STEPS, COARSE, LANES), F32), sds((3, CAP, LANES), F32)),
        in_specs=[VMEM, pl.BlockSpec(memory_space=pl.ANY)],
        out_specs=(VMEM, VMEM),
        compiler_params=limits(63),
        cost_estimate=pl.CostEstimate(flops=300_000_000, bytes_accessed=2_700_000, transcendentals=0),
        name="receive_rows",
    )(got, ends)
    coarse_north = ring(coarse, "ny", -1)
    coarse_south = ring(coarse, "ny", 1)
    north_flag = lax.axis_index("ny") < lax.axis_size("ny") - 1
    tall = jnp.concatenate(
        [coarse_south[:, 8:], coarse, jnp.where(north_flag, coarse_north[:, :8], 0.0)], axis=1
    )

    side_state, side_coef = pl.pallas_call(
        side_strips_kernel,
        out_shape=(frame(3, 2), frame(STEPS, 5, 2)),
        in_specs=[SMEM] + [VMEM] * 3 + [pl.BlockSpec(memory_space=pl.ANY)],
        out_specs=(VMEM, VMEM),
        scratch_shapes=[
            pltpu.VMEM((FTILE, FR + 8, LANES), F32),
            pltpu.VMEM((STEPS * FTILE, FR + 8, LANES), F32),
        ],
        compiler_params=limits(PREPARE_MIB),
        cost_estimate=pl.CostEstimate(flops=12_000_000, bytes_accessed=6_000_000, transcendentals=0),
        name="side_strips",
    )(shifts, ends, from_east, from_west, coarse)
    tall_east = ring(tall, "nx", -1)
    tall_west = ring(tall, "nx", 1)

    return pl.pallas_call(
        steps_kernel,
        out_shape=(sds((ROWS, COLS), F32),) * 3,
        in_specs=[SMEM] + [pl.BlockSpec(memory_space=pl.ANY)] * 5 + [VMEM] * 4,
        out_specs=(VMEM,) * 3,
        scratch_shapes=[
            pltpu.VMEM((3, FTILE, FR + 8, LANES), F32),
            pltpu.VMEM((3, FTILE, FR + 8, LANES), F32),
            pltpu.VMEM((STEPS, 5, FTILE - 2, FR, LANES), F32),
            pltpu.VMEM((STEPS, 5, 2, FR, LANES), F32),
            pltpu.VMEM((STEPS, 2 * LANES, FC), BF16),
            pltpu.SemaphoreType.DMA((9 + 3 * STEPS,)),
        ],
        compiler_params=limits(STEPS_MIB),
        cost_estimate=pl.CostEstimate(
            flops=400_000_000, bytes_accessed=23_000_000, transcendentals=0
        ),
        name="steps",
    )(shifts, mid_state, side_state, mid_coef, side_coef, cols, tall, tall_east, tall_west, edge)


def solution(mesh):
    in_specs = (
        P("ny", "nx"),
        P("ny", "nx"),
        P("ny", "nx"),
        P("ny", "nx"),
        P(None, "ny", "nx"),
        P(),
        P(None, ("ny", "nx"), None),
        P(None, ("ny", "nx")),
        P(None, ("ny", "nx")),
        P(None, "ny"),
        P(None, "nx", "ny"),
    )
    out_specs = (P("ny", "nx"), P("ny", "nx"), P("ny", "nx"))
    return jax.shard_map(local, mesh=mesh, in_specs=in_specs, out_specs=out_specs, check_vma=False)
```

time: 123 us -> 111 us (0.902)
  local copies, waits for them, and re-layouts: 24 us -> 1.96 us
  Pallas kernels: 37.7 us -> 48.4 us
  waiting for transfers between devices: 26.2 us -> 32.8 us
  other arithmetic: 5.9 us -> 0.77 us
  starting transfers between devices: 27.9 us -> 25.7 us
    unnamed x41 -> x16, local copies, waits for them, and re-layouts: 22.7 us -> 1.96 us
    all_to_all x1, waiting for transfers between devices: 0.01 us -> 19.8 us  [local(): lax.all_to_all(send, ('ny', 'nx'), split_axis=0, concat_axis=0, tiled=True)]
    ppermute x8, waiting for transfers between devices: 26.2 us -> 13 us  [ring(): lax.ppermute(value, axis, [(i, (i + by) % count) for i in range(count)])]
    pallas_call x3 -> x4, Pallas kernels: 32.6 us -> 40.8 us  [the longest x1 16.6 us: local(): pl.pallas_call(steps_kernel, out_shape=(sds((ROWS, COLS), F32),) * 3, in_...]
    unnamed x7 -> x0, other arithmetic: 4.52 us -> none
    pallas_call x1, Pallas kernels: 1.93 us -> 4.61 us  [local(): pl.pallas_call(pack_kernel, out_shape=sds((owners, CHUNK, LANES), F32), i...]
    ppermute x8, starting transfers between devices: 16.3 us -> 14.1 us  [ring(): lax.ppermute(value, axis, [(i, (i + by) % count) for i in range(count)])]
  transfers between devices with their start and end apart: 9 -> 9, of which waited for: 3 -> 4; matrix products, arithmetic and copies ran while one was open for 13% -> 1% of each run, Pallas kernels for 12% -> 24%
where the time goes in v1:
time: 111 us; the launch traced here: 110 us
  Pallas kernels  48.4 us (44%)
  waiting for transfers between devices  32.8 us (30%)
  starting transfers between devices  25.7 us (23%)
  local copies, waits for them, and re-layouts  1.96 us (2%)
    all_to_all x1, waiting for transfers between devices, local(): lax.all_to_all(send, ('ny', 'nx'), split_axis=0, concat_axis=0, tiled=True)  19.8 us
    pallas_call x1, Pallas kernels, local(): pl.pallas_call(steps_kernel, out_shape=(sds((ROWS, COLS), F32),) * 3, in_...  16.6 us
    pallas_call x1, Pallas kernels, local(): pl.pallas_call(prepare_kernel, out_shape=(frame(3, FTILE - 2), frame(STEP...  15.1 us
    ppermute x8, starting transfers between devices, ring(): lax.ppermute(value, axis, [(i, (i + by) % count) for i in range(count)])  14.1 us
    ppermute x8, waiting for transfers between devices, ring(): lax.ppermute(value, axis, [(i, (i + by) % count) for i in range(count)])  13 us
    all_to_all x1, starting transfers between devices, local(): lax.all_to_all(send, ('ny', 'nx'), split_axis=0, concat_axis=0, tiled=True)  11.6 us
    pallas_call x1, Pallas kernels, local(): pl.pallas_call(side_strips_kernel, out_shape=(frame(3, 2), frame(STEPS, 5...  6.49 us
    pallas_call x1, Pallas kernels, local(): pl.pallas_call(pack_kernel, out_shape=sds((owners, CHUNK, LANES), F32), i...  4.61 us
  transfers between devices with their start and end apart: 9, of which 4 were waited for; matrix products, arithmetic and copies ran while one was open for 1% of the time, Pallas kernels for 24%

profile of v1, /device:TPU:0, one launch (start us, length us, event | category | flops | bytes accessed | tf_op | source)
XLA Modules:
  0.0 110.5 jit_solution(6686719928956946985)
XLA Ops:
  0.6 2.6 %messages.1 = (f32[232,1152]{1,0:T(8,128)}, f32[64,1152]{1,0:T(8,128)}) custom-call(f32[144,1152]{1,0:T(8,128)} %e_ref.1, f32[144,1152]{1,0:T(8,128)} %u_ref.1, f32[144,1152]{1,0:T(8,128)} %v_ref.1, f32[144,1152]{1,0:T(8,128)} %b_ref.1, s32[4,144,1152]{2,1,0:T(8,128)} %m_ref.1, f32[144,1152]{1,0:T(8,128)} %e_ref.1, f32[144,1152]{1,0:T(8,128)} %u_ref.1, ...), custom_call_target="tpu_custom_call" | custom-call | flops 300000 | bytes 2700000 | tf_op jit(solution)/shard_map/messages/pallas_call | solution.py:482
  3.3 2.3 %collective-permute-start.1 = (f32[232,1152]{1,0:T(8,128)}, f32[232,1152]{1,0:T(8,128)}, u32[]{:S(2)}, u32[]{:S(2)}) collective-permute-start(f32[232,1152]{1,0:T(8,128)} %get-tuple-element.19), channel_id=1, source_target_pairs={{0,112},{16,0},{32,16},{48,32},{64,48},{80,64},{96,80},{112,96},{1... | collective-permute-start | bytes 3207176 | tf_op jit(solution)/shard_map/ppermute | solution.py:465
  5.6 0.0 collective-permute-start
  5.6 4.6 %pack_rows.1 = f32[128,40,128]{2,1,0:T(8,128)} custom-call(s32[1,4]{1,0:T(1,128)} %bitcast.5, s32[4,256]{1,0:T(4,128)} %dest_ref.1, s32[4,256]{1,0:T(4,128)} %coarse_ref.1, f32[4,256,128]{2,1,0:T(8,128)} %vals_ref.1, f32[4,1,144]{2,1,0:T(1,128)} %panel_ref.1, f32[64,1152]{1,0:T(8,128)} %get-tuple-element.18.after_ref), custom_call_target="tpu_custom_call" | custom-call | flops 800000000 | bytes 3200000 | tf_op jit(solution)/shard_map/pack_rows/pallas_call | solution.py:498
  10.2 3.0 %collective-permute-done.south_ref = f32[64,1152]{1,0:T(8,128)S(1)} collective-permute-done((f32[64,1152]{1,0:T(8,128)}, f32[64,1152]{1,0:T(8,128)S(1)}, u32[]{:S(2)}, u32[]{:S(2)}) %collective-permute-start) | collective-permute-done | bytes 294944 | tf_op jit(solution)/shard_map/ppermute | solution.py:465
  13.1 5.3 %collective-permute-done.1.north_ref = f32[232,1152]{1,0:T(8,128)} collective-permute-done((f32[232,1152]{1,0:T(8,128)}, f32[232,1152]{1,0:T(8,128)}, u32[]{:S(2)}, u32[]{:S(2)}) %collective-permute-start.1) | collective-permute-done | bytes 1069088 | tf_op jit(solution)/shard_map/ppermute | solution.py:465
  18.4 11.6 %all-to-all-start = ((f32[128,40,128]{2,1,0:T(8,128)}), f32[128,40,128]{2,1,0:T(8,128)}, u32[]{:S(2)}, u32[]{:S(2)}) async-start(f32[128,40,128]{2,1,0:T(8,128)} %pack_rows.1), calls=%async_computation | async-start | bytes 5242880 | tf_op jit(solution)/shard_map/all_to_all | solution.py:508
  30.0 15.1 %prepare.1 = (f32[3,8,152,128]{3,2,1,0:T(8,128)}, f32[4,5,8,152,128]{4,3,2,1,0:T(8,128)}, bf16[4,256,1280]{2,1,0:T(8,128)(2,1)}, f32[8,3,200,128]{3,2,1,0:T(8,12...) custom-call(s32[2,4]{1,0:T(2,128)} %bitcast.2, f32[144,1152]{1,0:T(8,128)} %e_ref.1, f32[144,1152]{1,0:T(8,128)} %u_ref.1, ...), custom_call_target="tpu_custom_call" | custom-call | flops 60000000 | bytes 27000000 | tf_op jit(solution)/shard_map/prepare/pallas_call | solution.py:512
  45.2 0.0 copy-start.6
  45.2 19.8 %all-to-all-done.got_ref = f32[128,40,128]{2,1,0:T(8,128)} async-done(((f32[128,40,128]{2,1,0:T(8,128)}), f32[128,40,128]{2,1,0:T(8,128)}, u32[]{:S(2)}, u32[]{:S(2)}) %all-to-all-start) | async-done | bytes 2621472 | tf_op jit(solution)/shard_map/all_to_all | solution.py:508
  65.0 2.9 %receive_rows.1 = (f32[4,16,128]{2,1,0:T(8,128)}, f32[3,8,128]{2,1,0:T(8,128)}) custom-call(f32[128,40,128]{2,1,0:T(8,128)} %all-to-all-done.got_ref, f32[8,3,200,128]{3,2,1,0:T(8,128)} %get-tuple-element.23.after_ref.ends_ref), custom_call_target="tpu_custom_call" | custom-call | flops 300000000 | bytes 2700000 | tf_op jit(solution)/shard_map/receive_rows/pallas_call | solution.py:538
  67.9 1.2 %collective-permute-start.5 = (f32[4,16,128]{2,1,0:T(8,128)}, f32[4,16,128]{2,1,0:T(8,128)S(1)}, u32[]{:S(2)}, u32[]{:S(2)}) collective-permute-start(f32[4,16,128]{2,1,0:T(8,128)} %get-tuple-element.27.after_ref), channel_id=1, source_target_pairs={{0,112},{16,0},{32,16},{48,32},{64,48},{80,64},{96,80},{112,96},{1... | collective-permute-start | bytes 98312 | tf_op jit(solution)/shard_map/ppermute | solution.py:465
  69.1 0.2 collective-permute-start.3
  69.2 5.2 %collective-permute-start.2 = (f32[3,152,128]{2,1,0:T(8,128)S(1)}, f32[3,152,128]{2,1,0:T(8,128)S(1)}, u32[]{:S(2)}, u32[]{:S(2)}) collective-permute-start(f32[3,152,128]{2,1,0:T(8,128)S(1)} %copy-done.6), channel_id=1, source_target_pairs={{0,15},{1,0},{2,1},{3,2},{4,3},{5,4},{6,5},{7,6},{8,7},{9,8},{10,9... | collective-permute-start | bytes 700424 | tf_op jit(solution)/shard_map/ppermute | solution.py:465
  74.4 4.7 %collective-permute-done.4 = f32[4,16,128]{2,1,0:T(8,128)S(1)} collective-permute-done((f32[4,16,128]{2,1,0:T(8,128)}, f32[4,16,128]{2,1,0:T(8,128)S(1)}, u32[]{:S(2)}, u32[]{:S(2)}) %collective-permute-start.4) | collective-permute-done | bytes 32800 | tf_op jit(solution)/shard_map/ppermute | solution.py:465
  79.2 0.8 pad_maximum_fusion.own_ref
  79.9 0.0 collective-permute-start.7
  80.0 5.3 %collective-permute-start.6 = (f32[4,32,128]{2,1,0:T(8,128)S(1)}, f32[4,32,128]{2,1,0:T(8,128)S(1)}, u32[]{:S(2)}, u32[]{:S(2)}) collective-permute-start(f32[4,32,128]{2,1,0:T(8,128)S(1)} %pad_maximum_fusion.own_ref), channel_id=1, source_target_pairs={{0,15},{1,0},{2,1},{3,2},{4,3},{5,4},{6,5},{7,6},{8,7},{9,8},{10,9... | collective-permute-start | bytes 196616 | tf_op jit(solution)/shard_map/ppermute | solution.py:465
  85.3 0.6 copy-done.3
  85.9 0.7 copy-done.2
  86.6 6.5 %side_strips.1 = (f32[3,2,152,128]{3,2,1,0:T(8,128)}, f32[4,5,2,152,128]{4,3,2,1,0:T(8,128)}) custom-call(s32[2,4]{1,0:T(2,128)} %bitcast.3, f32[8,3,200,128]{3,2,1,0:T(8,128)} %get-tuple-element.23.after_ref.ends_ref, f32[3,152,128]{2,1,0:T(8,128)} %copy-done.2, f32[152,128]{1,0:T(8,128)} %copy-done.3, f32[4,16,128]{2,1,0:T(8,128)} %get-tuple-element.27.after_ref), custom_call_target="tpu_custom_call" | custom-call | flops 12000000 | bytes 6000000 | tf_op jit(solution)/shard_map/side_strips/pallas_call | solution.py:554
  93.1 0.6 copy-done.4
  93.7 0.0 copy-done.5
  93.8 16.6 %steps.1 = (f32[144,1152]{1,0:T(8,128)}, f32[144,1152]{1,0:T(8,128)}, f32[144,1152]{1,0:T(8,128)}) custom-call(s32[2,4]{1,0:T(2,128)} %bitcast.4, f32[3,8,152,128]{3,2,1,0:T(8,128)} %get-tuple-element.22.mid_state, f32[3,2,152,128]{3,2,1,0:T(8,128)} %get-tuple-element.28.side_state, f32[4,5,8,152,128]{4,3,2,1,0:T(8,128)} %get-tuple-element.29.mid_hbm, ...), custom_call_target="tpu_custom_call" | custom-call | flops 400000000 | bytes 23000000 | tf_op jit(solution)/shard_map/steps/pallas_call | solution.py:570
  (19 shorter events, 0.0 us)
Async XLA Ops:
  3.3 15.1 %collective-permute-start.1 = (f32[232,1152]{1,0:T(8,128)}, f32[232,1152]{1,0:T(8,128)}, u32[]{:S(2)}, u32[]{:S(2)}) collective-permute-start(f32[232,1152]{1,0:T(8,128)} %get-tuple-element.19), channel_id=1, source_target_pairs={{0,112},{16,0},{32,16},{48,32},{64,48},{80,64},{96,80},{112,96},{1... | collective-permute-start | bytes 3207176 | tf_op jit(solution)/shard_map/ppermute | solution.py:465
  5.6 7.6 %collective-permute-start = (f32[64,1152]{1,0:T(8,128)}, f32[64,1152]{1,0:T(8,128)S(1)}, u32[]{:S(2)}, u32[]{:S(2)}) collective-permute-start(f32[64,1152]{1,0:T(8,128)} %get-tuple-element.18.after_ref), channel_id=1, source_target_pairs={{0,16},{16,32},{32,48},{48,64},{64,80},{80,96},{96,112},{112,0},{1... | collective-permute-start | bytes 884744 | tf_op jit(solution)/shard_map/ppermute | solution.py:465
  13.1 16.9 %copy-start = (f32[64,1152]{1,0:T(8,128)}, f32[64,1152]{1,0:T(8,128)S(1)}, u32[]{:S(2)}) copy-start(f32[64,1152]{1,0:T(8,128)S(1)} %collective-permute-done.south_ref) | copy-start | bytes 884740
  18.4 46.6 %all-to-all-start = ((f32[128,40,128]{2,1,0:T(8,128)}), f32[128,40,128]{2,1,0:T(8,128)}, u32[]{:S(2)}, u32[]{:S(2)}) async-start(f32[128,40,128]{2,1,0:T(8,128)} %pack_rows.1), calls=%async_computation | async-start | bytes 5242880 | tf_op jit(solution)/shard_map/all_to_all | solution.py:508
  45.2 23.9 %copy-start.7 = (f32[152,128]{1,0:T(8,128)S(1)}, f32[152,128]{1,0:T(8,128)}, u32[]{:S(2)}) copy-start(f32[152,128]{1,0:T(8,128)} %get-tuple-element.25) | copy-start | bytes 233476
  45.2 24.0 %copy-start.6 = (f32[3,152,128]{2,1,0:T(8,128)S(1)}, f32[3,152,128]{2,1,0:T(8,128)}, u32[]{:S(2)}) copy-start(f32[3,152,128]{2,1,0:T(8,128)} %get-tuple-element.24) | copy-start | bytes 700420
  67.9 6.5 %collective-permute-start.5 = (f32[4,16,128]{2,1,0:T(8,128)}, f32[4,16,128]{2,1,0:T(8,128)S(1)}, u32[]{:S(2)}, u32[]{:S(2)}) collective-permute-start(f32[4,16,128]{2,1,0:T(8,128)} %get-tuple-element.27.after_ref), channel_id=1, source_target_pairs={{0,112},{16,0},{32,16},{48,32},{64,48},{80,64},{96,80},{112,96},{1... | collective-permute-start | bytes 98312 | tf_op jit(solution)/shard_map/ppermute | solution.py:465
  69.1 16.2 %collective-permute-start.3 = (f32[152,128]{1,0:T(8,128)S(1)}, f32[152,128]{1,0:T(8,128)S(1)}, u32[]{:S(2)}, u32[]{:S(2)}) collective-permute-start(f32[152,128]{1,0:T(8,128)S(1)} %copy-done.7), channel_id=1, source_target_pairs={{0,1},{1,2},{2,3},{3,4},{4,5},{5,6},{6,7},{7,8},{8,9},{9,10},{10,1... | collective-permute-start | bytes 233480 | tf_op jit(solution)/shard_map/ppermute | solution.py:465
  69.2 16.1 %collective-permute-start.2 = (f32[3,152,128]{2,1,0:T(8,128)S(1)}, f32[3,152,128]{2,1,0:T(8,128)S(1)}, u32[]{:S(2)}, u32[]{:S(2)}) collective-permute-start(f32[3,152,128]{2,1,0:T(8,128)S(1)} %copy-done.6), channel_id=1, source_target_pairs={{0,15},{1,0},{2,1},{3,2},{4,3},{5,4},{6,5},{7,6},{8,7},{9,8},{10,9... | collective-permute-start | bytes 700424 | tf_op jit(solution)/shard_map/ppermute | solution.py:465
  74.4 4.8 %collective-permute-start.4 = (f32[4,16,128]{2,1,0:T(8,128)}, f32[4,16,128]{2,1,0:T(8,128)S(1)}, u32[]{:S(2)}, u32[]{:S(2)}) collective-permute-start(f32[4,16,128]{2,1,0:T(8,128)} %get-tuple-element.27.after_ref), channel_id=1, source_target_pairs={{0,16},{16,32},{32,48},{48,64},{64,80},{80,96},{96,112},{112,0},{1... | collective-permute-start | bytes 98312 | tf_op jit(solution)/shard_map/ppermute | solution.py:465
  79.9 13.2 %copy-start.1 = (f32[4,32,128]{2,1,0:T(8,128)}, f32[4,32,128]{2,1,0:T(8,128)S(1)}, u32[]{:S(2)}) copy-start(f32[4,32,128]{2,1,0:T(8,128)S(1)} %pad_maximum_fusion.own_ref) | copy-start | bytes 196612
  79.9 13.2 %collective-permute-start.7 = (f32[4,32,128]{2,1,0:T(8,128)S(1)}, f32[4,32,128]{2,1,0:T(8,128)S(1)}, u32[]{:S(2)}, u32[]{:S(2)}) collective-permute-start(f32[4,32,128]{2,1,0:T(8,128)S(1)} %pad_maximum_fusion.own_ref), channel_id=1, source_target_pairs={{0,1},{1,2},{2,3},{3,4},{4,5},{5,6},{6,7},{7,8},{8,9},{9,10},{10,1... | collective-permute-start | bytes 196616 | tf_op jit(solution)/shard_map/ppermute | solution.py:465
  80.0 13.2 %collective-permute-start.6 = (f32[4,32,128]{2,1,0:T(8,128)S(1)}, f32[4,32,128]{2,1,0:T(8,128)S(1)}, u32[]{:S(2)}, u32[]{:S(2)}) collective-permute-start(f32[4,32,128]{2,1,0:T(8,128)S(1)} %pad_maximum_fusion.own_ref), channel_id=1, source_target_pairs={{0,15},{1,0},{2,1},{3,2},{4,3},{5,4},{6,5},{7,6},{8,7},{9,8},{10,9... | collective-permute-start | bytes 196616 | tf_op jit(solution)/shard_map/ppermute | solution.py:465
  85.3 0.6 copy-start.3
  85.9 0.7 copy-start.2
  93.1 0.6 copy-start.4
  93.1 0.6 copy-start.5

commit v2 on v1

--- a/solution.py
+++ b/solution.py
@@ -432,9 +432,8 @@
         )
     for copy in copies:
         copy.start()
-    for each in per_step:
-        for copy in each:
-            copy.start()
+    for copy in per_step[0]:
+        copy.start()
     for f in range(3):
         for k in range(FTILE):
             even[f, k, FR:, :] = jnp.zeros((8, LANES), F32)
@@ -445,6 +444,9 @@
     for s in range(STEPS):
         for copy in per_step[s]:
             copy.wait()
+        if s + 1 < STEPS:
+            for copy in per_step[s + 1]:
+                copy.start()
         one_step(
             s, shifts_ref, mid_ref, side_ref, cols_ref, own_ref, east_ref, west_ref, edge_ref,
             cur, new,
@@ -546,11 +548,6 @@
     )(got, ends)
     coarse_north = ring(coarse, "ny", -1)
     coarse_south = ring(coarse, "ny", 1)
-    north_flag = lax.axis_index("ny") < lax.axis_size("ny") - 1
-    tall = jnp.concatenate(
-        [coarse_south[:, 8:], coarse, jnp.where(north_flag, coarse_north[:, :8], 0.0)], axis=1
-    )
-
     side_state, side_coef = pl.pallas_call(
         side_strips_kernel,
         out_shape=(frame(3, 2), frame(STEPS, 5, 2)),
@@ -564,6 +561,13 @@
         cost_estimate=pl.CostEstimate(flops=12_000_000, bytes_accessed=6_000_000, transcendentals=0),
         name="side_strips",
     )(shifts, ends, from_east, from_west, coarse)
+    coarse_north, coarse_south, side_state = lax.optimization_barrier(
+        (coarse_north, coarse_south, side_state)
+    )
+    north_flag = lax.axis_index("ny") < lax.axis_size("ny") - 1
+    tall = jnp.concatenate(
+        [coarse_south[:, 8:], coarse, jnp.where(north_flag, coarse_north[:, :8], 0.0)], axis=1
+    )
     tall_east = ring(tall, "nx", -1)
     tall_west = ring(tall, "nx", 1)
 

time: 111 us -> 104 us (0.937)
  waiting for transfers between devices: 32.8 us -> 25.3 us
  starting transfers between devices: 25.7 us -> 27.4 us
    all_to_all x1, waiting for transfers between devices: 19.8 us -> 14.8 us  [local(): lax.all_to_all(send, ('ny', 'nx'), split_axis=0, concat_axis=0, tiled=True)]
    ppermute x8, waiting for transfers between devices: 13 us -> 10.5 us  [ring(): lax.ppermute(value, axis, [(i, (i + by) % count) for i in range(count)])]
    ppermute x8, starting transfers between devices: 14.1 us -> 15.7 us  [ring(): lax.ppermute(value, axis, [(i, (i + by) % count) for i in range(count)])]
  transfers between devices with their start and end apart: 9 -> 9, of which waited for: 4 -> 4; matrix products, arithmetic and copies ran while one was open for 1% -> 0% of each run, Pallas kernels for 24% -> 28%
where the time goes in v2:
time: 104 us
  Pallas kernels  48.2 us (46%)
  starting transfers between devices  27.4 us (26%)
  waiting for transfers between devices  25.3 us (24%)
  local copies, waits for them, and re-layouts  1.97 us (2%)
    pallas_call x1, Pallas kernels, local(): pl.pallas_call(steps_kernel, out_shape=(sds((ROWS, COLS), F32),) * 3, in_...  16.6 us
    ppermute x8, starting transfers between devices, ring(): lax.ppermute(value, axis, [(i, (i + by) % count) for i in range(count)])  15.7 us
    pallas_call x1, Pallas kernels, local(): pl.pallas_call(prepare_kernel, out_shape=(frame(3, FTILE - 2), frame(STEP...  15.1 us
    all_to_all x1, waiting for transfers between devices, local(): lax.all_to_all(send, ('ny', 'nx'), split_axis=0, concat_axis=0, tiled=True)  14.8 us
    all_to_all x1, starting transfers between devices, local(): lax.all_to_all(send, ('ny', 'nx'), split_axis=0, concat_axis=0, tiled=True)  11.6 us
    ppermute x8, waiting for transfers between devices, ring(): lax.ppermute(value, axis, [(i, (i + by) % count) for i in range(count)])  10.5 us
    pallas_call x1, Pallas kernels, local(): pl.pallas_call(side_strips_kernel, out_shape=(frame(3, 2), frame(STEPS, 5...  6.41 us
    pallas_call x1, Pallas kernels, local(): pl.pallas_call(pack_kernel, out_shape=sds((owners, CHUNK, LANES), F32), i...  4.6 us
  transfers between devices with their start and end apart: 9, of which 4 were waited for; matrix products, arithmetic and copies ran while one was open for 0% of the time, Pallas kernels for 28%

profile of v2, /device:TPU:0, one launch (start us, length us, event | category | flops | bytes accessed | tf_op | source)
XLA Modules:
  0.0 103.8 jit_solution(15471883044039464440)
XLA Ops:
  0.6 2.6 %messages.1 = (f32[232,1152]{1,0:T(8,128)}, f32[64,1152]{1,0:T(8,128)}) custom-call(f32[144,1152]{1,0:T(8,128)} %e_ref.1, f32[144,1152]{1,0:T(8,128)} %u_ref.1, f32[144,1152]{1,0:T(8,128)} %v_ref.1, f32[144,1152]{1,0:T(8,128)} %b_ref.1, s32[4,144,1152]{2,1,0:T(8,128)} %m_ref.1, f32[144,1152]{1,0:T(8,128)} %e_ref.1, f32[144,1152]{1,0:T(8,128)} %u_ref.1, ...), custom_call_target="tpu_custom_call" | custom-call | flops 300000 | bytes 2700000 | tf_op jit(solution)/shard_map/messages/pallas_call | solution.py:484
  3.3 2.3 %collective-permute-start.1 = (f32[232,1152]{1,0:T(8,128)}, f32[232,1152]{1,0:T(8,128)}, u32[]{:S(2)}, u32[]{:S(2)}) collective-permute-start(f32[232,1152]{1,0:T(8,128)} %get-tuple-element.22), channel_id=1, source_target_pairs={{0,112},{16,0},{32,16},{48,32},{64,48},{80,64},{96,80},{112,96},{1... | collective-permute-start | bytes 3207176 | tf_op jit(solution)/shard_map/ppermute | solution.py:467
  5.6 4.6 %pack_rows.1 = f32[128,40,128]{2,1,0:T(8,128)} custom-call(s32[1,4]{1,0:T(1,128)} %bitcast.5, s32[4,256]{1,0:T(4,128)} %dest_ref.1, s32[4,256]{1,0:T(4,128)} %coarse_ref.1, f32[4,256,128]{2,1,0:T(8,128)} %vals_ref.1, f32[4,1,144]{2,1,0:T(1,128)} %panel_ref.1, f32[64,1152]{1,0:T(8,128)} %get-tuple-element.21.after_ref), custom_call_target="tpu_custom_call" | custom-call | flops 800000000 | bytes 3200000 | tf_op jit(solution)/shard_map/pack_rows/pallas_call | solution.py:500
  10.2 3.0 %collective-permute-done.south_ref = f32[64,1152]{1,0:T(8,128)S(1)} collective-permute-done((f32[64,1152]{1,0:T(8,128)}, f32[64,1152]{1,0:T(8,128)S(1)}, u32[]{:S(2)}, u32[]{:S(2)}) %collective-permute-start) | collective-permute-done | bytes 294944 | tf_op jit(solution)/shard_map/ppermute | solution.py:467
  13.1 5.3 %collective-permute-done.1.north_ref = f32[232,1152]{1,0:T(8,128)} collective-permute-done((f32[232,1152]{1,0:T(8,128)}, f32[232,1152]{1,0:T(8,128)}, u32[]{:S(2)}, u32[]{:S(2)}) %collective-permute-start.1) | collective-permute-done | bytes 1069088 | tf_op jit(solution)/shard_map/ppermute | solution.py:467
  18.4 11.6 %all-to-all-start = ((f32[128,40,128]{2,1,0:T(8,128)}), f32[128,40,128]{2,1,0:T(8,128)}, u32[]{:S(2)}, u32[]{:S(2)}) async-start(f32[128,40,128]{2,1,0:T(8,128)} %pack_rows.1), calls=%async_computation | async-start | bytes 5242880 | tf_op jit(solution)/shard_map/all_to_all | solution.py:510
  30.0 15.1 %prepare.1 = (f32[3,8,152,128]{3,2,1,0:T(8,128)}, f32[4,5,8,152,128]{4,3,2,1,0:T(8,128)}, bf16[4,256,1280]{2,1,0:T(8,128)(2,1)}, f32[8,3,200,128]{3,2,1,0:T(8,12...) custom-call(s32[2,4]{1,0:T(2,128)} %bitcast.2, f32[144,1152]{1,0:T(8,128)} %e_ref.1, f32[144,1152]{1,0:T(8,128)} %u_ref.1, ...), custom_call_target="tpu_custom_call" | custom-call | flops 60000000 | bytes 27000000 | tf_op jit(solution)/shard_map/prepare/pallas_call | solution.py:514
  45.2 5.1 %collective-permute-start.4 = (f32[3,152,128]{2,1,0:T(8,128)}, f32[3,152,128]{2,1,0:T(8,128)S(1)}, u32[]{:S(2)}, u32[]{:S(2)}) collective-permute-start(f32[3,152,128]{2,1,0:T(8,128)} %get-tuple-element.29), channel_id=1, source_target_pairs={{0,15},{1,0},{2,1},{3,2},{4,3},{5,4},{6,5},{7,6},{8,7},{9,8},{10,9... | collective-permute-start | bytes 700424 | tf_op jit(solution)/shard_map/ppermute | solution.py:467
  50.2 0.0 collective-permute-start.5
  50.2 14.8 %all-to-all-done.got_ref = f32[128,40,128]{2,1,0:T(8,128)} async-done(((f32[128,40,128]{2,1,0:T(8,128)}), f32[128,40,128]{2,1,0:T(8,128)}, u32[]{:S(2)}, u32[]{:S(2)}) %all-to-all-start) | async-done | bytes 2621472 | tf_op jit(solution)/shard_map/all_to_all | solution.py:510
  65.1 2.9 %receive_rows.1 = (f32[4,16,128]{2,1,0:T(8,128)}, f32[3,8,128]{2,1,0:T(8,128)}) custom-call(f32[128,40,128]{2,1,0:T(8,128)} %all-to-all-done.got_ref, f32[8,3,200,128]{3,2,1,0:T(8,128)} %get-tuple-element.27.after_ref.ends_ref), custom_call_target="tpu_custom_call" | custom-call | flops 300000000 | bytes 2700000 | tf_op jit(solution)/shard_map/receive_rows/pallas_call | solution.py:540
  68.0 3.0 %collective-permute-start.2 = (f32[4,16,128]{2,1,0:T(8,128)}, f32[4,16,128]{2,1,0:T(8,128)S(1)}, u32[]{:S(2)}, u32[]{:S(2)}) collective-permute-start(f32[4,16,128]{2,1,0:T(8,128)} %get-tuple-element.28.after_ref), channel_id=1, source_target_pairs={{0,112},{16,0},{32,16},{48,32},{64,48},{80,64},{96,80},{112,96},{1... | collective-permute-start | bytes 98312 | tf_op jit(solution)/shard_map/ppermute | solution.py:467
  70.9 0.0 collective-permute-done.5.west_ref
  70.9 0.0 collective-permute-done.4.east_ref
  70.9 0.6 copy-done.4
  71.6 0.7 copy-done.2
  72.3 6.4 %side_strips.1 = (f32[3,2,152,128]{3,2,1,0:T(8,128)}, f32[4,5,2,152,128]{4,3,2,1,0:T(8,128)}) custom-call(s32[2,4]{1,0:T(2,128)} %bitcast.3, f32[8,3,200,128]{3,2,1,0:T(8,128)} %get-tuple-element.27.after_ref.ends_ref, f32[3,152,128]{2,1,0:T(8,128)} %copy-done.2, f32[152,128]{1,0:T(8,128)} %copy-done.4, f32[4,16,128]{2,1,0:T(8,128)} %get-tuple-element.28.after_ref), custom_call_target="tpu_custom_call" | custom-call | flops 12000000 | bytes 6000000 | tf_op jit(solution)/shard_map/side_strips/pallas_call | solution.py:551
  78.7 0.0 collective-permute-done.2
  78.7 0.5 collective-permute-start.7
  79.3 4.9 %collective-permute-start.6 = (f32[4,32,128]{2,1,0:T(8,128)S(1)}, f32[4,32,128]{2,1,0:T(8,128)S(1)}, u32[]{:S(2)}, u32[]{:S(2)}) collective-permute-start(f32[4,32,128]{2,1,0:T(8,128)S(1)} %pad_maximum_fusion.own_ref), channel_id=1, source_target_pairs={{0,15},{1,0},{2,1},{3,2},{4,3},{5,4},{6,5},{7,6},{8,7},{9,8},{10,9... | collective-permute-start | bytes 196616 | tf_op jit(solution)/shard_map/ppermute | solution.py:467
  84.2 2.2 %collective-permute-done.7.west_ref = f32[4,32,128]{2,1,0:T(8,128)S(1)} collective-permute-done((f32[4,32,128]{2,1,0:T(8,128)S(1)}, f32[4,32,128]{2,1,0:T(8,128)S(1)}, u32[]{:S(2)}, u32[]{:S(2)}) %collective-permute-start.7) | collective-permute-done | bytes 65568 | tf_op jit(solution)/shard_map/ppermute | solution.py:467
  86.4 0.6 copy-done.5
  87.0 0.0 copy-done.6
  87.1 16.6 %steps.1 = (f32[144,1152]{1,0:T(8,128)}, f32[144,1152]{1,0:T(8,128)}, f32[144,1152]{1,0:T(8,128)}) custom-call(s32[2,4]{1,0:T(2,128)} %bitcast.4, f32[3,8,152,128]{3,2,1,0:T(8,128)} %get-tuple-element.25.mid_state, f32[3,2,152,128]{3,2,1,0:T(8,128)} %get-tuple-element.32.side_state, f32[4,5,8,152,128]{4,3,2,1,0:T(8,128)} %get-tuple-element.33.mid_hbm, ...), custom_call_target="tpu_custom_call" | custom-call | flops 400000000 | bytes 23000000 | tf_op jit(solution)/shard_map/steps/pallas_call | solution.py:574
  (17 shorter events, 0.0 us)
Async XLA Ops:
  3.3 15.1 %collective-permute-start.1 = (f32[232,1152]{1,0:T(8,128)}, f32[232,1152]{1,0:T(8,128)}, u32[]{:S(2)}, u32[]{:S(2)}) collective-permute-start(f32[232,1152]{1,0:T(8,128)} %get-tuple-element.22), channel_id=1, source_target_pairs={{0,112},{16,0},{32,16},{48,32},{64,48},{80,64},{96,80},{112,96},{1... | collective-permute-start | bytes 3207176 | tf_op jit(solution)/shard_map/ppermute | solution.py:467
  5.6 7.6 %collective-permute-start = (f32[64,1152]{1,0:T(8,128)}, f32[64,1152]{1,0:T(8,128)S(1)}, u32[]{:S(2)}, u32[]{:S(2)}) collective-permute-start(f32[64,1152]{1,0:T(8,128)} %get-tuple-element.21.after_ref), channel_id=1, source_target_pairs={{0,16},{16,32},{32,48},{48,64},{64,80},{80,96},{96,112},{112,0},{1... | collective-permute-start | bytes 884744 | tf_op jit(solution)/shard_map/ppermute | solution.py:467
  13.1 16.9 %copy-start = (f32[64,1152]{1,0:T(8,128)}, f32[64,1152]{1,0:T(8,128)S(1)}, u32[]{:S(2)}) copy-start(f32[64,1152]{1,0:T(8,128)S(1)} %collective-permute-done.south_ref) | copy-start | bytes 884740
  18.4 46.7 %all-to-all-start = ((f32[128,40,128]{2,1,0:T(8,128)}), f32[128,40,128]{2,1,0:T(8,128)}, u32[]{:S(2)}, u32[]{:S(2)}) async-start(f32[128,40,128]{2,1,0:T(8,128)} %pack_rows.1), calls=%async_computation | async-start | bytes 5242880 | tf_op jit(solution)/shard_map/all_to_all | solution.py:510
  45.2 25.8 %collective-permute-start.4 = (f32[3,152,128]{2,1,0:T(8,128)}, f32[3,152,128]{2,1,0:T(8,128)S(1)}, u32[]{:S(2)}, u32[]{:S(2)}) collective-permute-start(f32[3,152,128]{2,1,0:T(8,128)} %get-tuple-element.29), channel_id=1, source_target_pairs={{0,15},{1,0},{2,1},{3,2},{4,3},{5,4},{6,5},{7,6},{8,7},{9,8},{10,9... | collective-permute-start | bytes 700424 | tf_op jit(solution)/shard_map/ppermute | solution.py:467
  50.2 20.7 %collective-permute-start.5 = (f32[152,128]{1,0:T(8,128)}, f32[152,128]{1,0:T(8,128)S(1)}, u32[]{:S(2)}, u32[]{:S(2)}) collective-permute-start(f32[152,128]{1,0:T(8,128)} %get-tuple-element.30), channel_id=1, source_target_pairs={{0,1},{1,2},{2,3},{3,4},{4,5},{5,6},{6,7},{7,8},{8,9},{9,10},{10,1... | collective-permute-start | bytes 233480 | tf_op jit(solution)/shard_map/ppermute | solution.py:467
  68.0 10.7 %copy-start.3 = (f32[4,16,128]{2,1,0:T(8,128)S(1)}, f32[4,16,128]{2,1,0:T(8,128)}, u32[]{:S(2)}) copy-start(f32[4,16,128]{2,1,0:T(8,128)} %get-tuple-element.28.after_ref) | copy-start | bytes 98308
  68.0 10.7 %collective-permute-start.3 = (f32[4,16,128]{2,1,0:T(8,128)}, f32[4,16,128]{2,1,0:T(8,128)S(1)}, u32[]{:S(2)}, u32[]{:S(2)}) collective-permute-start(f32[4,16,128]{2,1,0:T(8,128)} %get-tuple-element.28.after_ref), channel_id=1, source_target_pairs={{0,16},{16,32},{32,48},{48,64},{64,80},{80,96},{96,112},{112,0},{1... | collective-permute-start | bytes 98312 | tf_op jit(solution)/shard_map/ppermute | solution.py:467
  68.0 10.7 %collective-permute-start.2 = (f32[4,16,128]{2,1,0:T(8,128)}, f32[4,16,128]{2,1,0:T(8,128)S(1)}, u32[]{:S(2)}, u32[]{:S(2)}) collective-permute-start(f32[4,16,128]{2,1,0:T(8,128)} %get-tuple-element.28.after_ref), channel_id=1, source_target_pairs={{0,112},{16,0},{32,16},{48,32},{64,48},{80,64},{96,80},{112,96},{1... | collective-permute-start | bytes 98312 | tf_op jit(solution)/shard_map/ppermute | solution.py:467
  70.9 0.6 copy-start.4
  71.6 0.7 copy-start.2
  78.7 7.7 %copy-start.1 = (f32[4,32,128]{2,1,0:T(8,128)}, f32[4,32,128]{2,1,0:T(8,128)S(1)}, u32[]{:S(2)}) copy-start(f32[4,32,128]{2,1,0:T(8,128)S(1)} %pad_maximum_fusion.own_ref) | copy-start | bytes 196612
  78.7 7.7 %collective-permute-start.7 = (f32[4,32,128]{2,1,0:T(8,128)S(1)}, f32[4,32,128]{2,1,0:T(8,128)S(1)}, u32[]{:S(2)}, u32[]{:S(2)}) collective-permute-start(f32[4,32,128]{2,1,0:T(8,128)S(1)} %pad_maximum_fusion.own_ref), channel_id=1, source_target_pairs={{0,1},{1,2},{2,3},{3,4},{4,5},{5,6},{6,7},{7,8},{8,9},{9,10},{10,1... | collective-permute-start | bytes 196616 | tf_op jit(solution)/shard_map/ppermute | solution.py:467
  79.3 7.1 %collective-permute-start.6 = (f32[4,32,128]{2,1,0:T(8,128)S(1)}, f32[4,32,128]{2,1,0:T(8,128)S(1)}, u32[]{:S(2)}, u32[]{:S(2)}) collective-permute-start(f32[4,32,128]{2,1,0:T(8,128)S(1)} %pad_maximum_fusion.own_ref), channel_id=1, source_target_pairs={{0,15},{1,0},{2,1},{3,2},{4,3},{5,4},{6,5},{7,6},{8,7},{9,8},{10,9... | collective-permute-start | bytes 196616 | tf_op jit(solution)/shard_map/ppermute | solution.py:467
  86.4 0.6 copy-start.5
  86.4 0.6 copy-start.6

commit v3 on v2

--- a/solution.py
+++ b/solution.py
@@ -51,16 +51,19 @@
     return lax.dot_general(a, b, (dims, ((), ())), preferred_element_type=F32)
 
 
-def message_kernel(
-    e_top, u_top, v_top, b_top, m_top, e_low, u_low, v_low, b_low, m_low, north_ref, south_ref
-):
+def north_kernel(e_top, u_top, v_top, b_top, m_top, north_ref):
     for f, ref in enumerate((e_top, u_top, v_top)):
         north_ref[N_E + NHALO * f : N_E + NHALO * (f + 1), :] = ref[...]
     north_ref[N_B : N_B + WIDTHS[0], :] = b_top[...]
+    for s in range(STEPS):
+        north_ref[N_M[s] : N_M[s] + WIDTHS[s], :] = m_top[s, : WIDTHS[s], :].astype(F32)
+
+
+def south_kernel(e_low, u_low, v_low, b_low, m_low, after_ref, south_ref):
+    del after_ref
     for f, ref in enumerate((e_low, u_low, v_low, b_low)):
         south_ref[8 * f : 8 * f + 8, :] = ref[...]
     for s in range(STEPS):
-        north_ref[N_M[s] : N_M[s] + WIDTHS[s], :] = m_top[s, : WIDTHS[s], :].astype(F32)
         south_ref[32 + 8 * s : 40 + 8 * s, :] = m_low[s].astype(F32)
 
 
@@ -481,19 +484,29 @@
     top = lambda rows: pl.BlockSpec((rows, COLS), lambda g: (0, 0))
     low = pl.BlockSpec((8, COLS), lambda g: (ROWS // 8 - 1, 0))
     fields = (elevation, flux_x, flux_y, depth, wet_mask)
-    north_message, south_message = pl.pallas_call(
-        message_kernel,
-        out_shape=(sds((N_ROWS, COLS), F32), sds((S_ROWS, COLS), F32)),
+    north_message = pl.pallas_call(
+        north_kernel,
+        out_shape=sds((N_ROWS, COLS), F32),
         grid=(1,),
         in_specs=[top(NHALO)] * 3
-        + [top(WIDTHS[0]), pl.BlockSpec((STEPS, WIDTHS[0], COLS), lambda g: (0, 0, 0))]
-        + [low] * 4
-        + [pl.BlockSpec((STEPS, 8, COLS), lambda g: (0, ROWS // 8 - 1, 0))],
-        out_specs=(top(N_ROWS), top(S_ROWS)),
+        + [top(WIDTHS[0]), pl.BlockSpec((STEPS, WIDTHS[0], COLS), lambda g: (0, 0, 0))],
+        out_specs=top(N_ROWS),
         compiler_params=limits(63),
-        cost_estimate=pl.CostEstimate(flops=300_000, bytes_accessed=2_700_000, transcendentals=0),
-        name="messages",
-    )(*fields, *fields)
+        cost_estimate=pl.CostEstimate(flops=300_000, bytes_accessed=2_200_000, transcendentals=0),
+        name="north_message",
+    )(*fields)
+    south_message = pl.pallas_call(
+        south_kernel,
+        out_shape=sds((S_ROWS, COLS), F32),
+        grid=(1,),
+        in_specs=[low] * 4
+        + [pl.BlockSpec((STEPS, 8, COLS), lambda g: (0, ROWS // 8 - 1, 0))]
+        + [pl.BlockSpec(memory_space=pl.ANY)],
+        out_specs=top(S_ROWS),
+        compiler_params=limits(63),
+        cost_estimate=pl.CostEstimate(flops=80_000, bytes_accessed=600_000, transcendentals=0),
+        name="south_message",
+    )(*fields, north_message)
     from_north = ring(north_message, "ny", -1)
     from_south = ring(south_message, "ny", 1)
 

time: 104 us -> 104 us (level)
  waiting for transfers between devices: 25.3 us -> 23.6 us
  Pallas kernels: 48.2 us -> 49.8 us
    ppermute x8, waiting for transfers between devices: 10.5 us -> 8.78 us  [ring(): lax.ppermute(value, axis, [(i, (i + by) % count) for i in range(count)])]
    pallas_call x1 -> x2, Pallas kernels: 2.64 us -> 4.18 us  [the longest x1 2.44 us: local(): pl.pallas_call(north_kernel, out_shape=sds((N_ROWS, COLS), F32), grid=(1,...]
  transfers between devices with their start and end apart: 9 -> 9, of which waited for: 4 -> 4; matrix products, arithmetic and copies ran while one was open for 0% -> 0% of each run, Pallas kernels for 28% -> 30%
where the time goes in v3:
time: 104 us
  Pallas kernels  49.8 us (48%)
  starting transfers between devices  27.4 us (26%)
  waiting for transfers between devices  23.6 us (23%)
  local copies, waits for them, and re-layouts  1.98 us (2%)
    pallas_call x1, Pallas kernels, local(): pl.pallas_call(steps_kernel, out_shape=(sds((ROWS, COLS), F32),) * 3, in_...  16.6 us
    ppermute x8, starting transfers between devices, ring(): lax.ppermute(value, axis, [(i, (i + by) % count) for i in range(count)])  15.7 us
    pallas_call x1, Pallas kernels, local(): pl.pallas_call(prepare_kernel, out_shape=(frame(3, FTILE - 2), frame(STEP...  15.1 us
    all_to_all x1, waiting for transfers between devices, local(): lax.all_to_all(send, ('ny', 'nx'), split_axis=0, concat_axis=0, tiled=True)  14.8 us
    all_to_all x1, starting transfers between devices, local(): lax.all_to_all(send, ('ny', 'nx'), split_axis=0, concat_axis=0, tiled=True)  11.6 us
    ppermute x8, waiting for transfers between devices, ring(): lax.ppermute(value, axis, [(i, (i + by) % count) for i in range(count)])  8.78 us
    pallas_call x1, Pallas kernels, local(): pl.pallas_call(side_strips_kernel, out_shape=(frame(3, 2), frame(STEPS, 5...  6.41 us
    pallas_call x1, Pallas kernels, local(): pl.pallas_call(pack_kernel, out_shape=sds((owners, CHUNK, LANES), F32), i...  4.59 us
  transfers between devices with their start and end apart: 9, of which 4 were waited for; matrix products, arithmetic and copies ran while one was open for 0% of the time, Pallas kernels for 30%

profile of v3, /device:TPU:0, one launch (start us, length us, event | category | flops | bytes accessed | tf_op | source)
XLA Modules:
  0.0 103.6 jit_solution(4134817308248821970)
XLA Ops:
  0.6 2.4 %north_message.1.after_ref = f32[232,1152]{1,0:T(8,128)} custom-call(f32[144,1152]{1,0:T(8,128)} %e_ref.1, f32[144,1152]{1,0:T(8,128)} %u_ref.1, f32[144,1152]{1,0:T(8,128)} %v_ref.1, f32[144,1152]{1,0:T(8,128)} %b_ref.1, s32[4,144,1152]{2,1,0:T(8,128)} %m_ref.1), custom_call_target="tpu_custom_call" | custom-call | flops 300000 | bytes 2200000 | tf_op jit(solution)/shard_map/north_message/pallas_call | solution.py:487
  3.1 2.3 %collective-permute-start.1 = (f32[232,1152]{1,0:T(8,128)}, f32[232,1152]{1,0:T(8,128)}, u32[]{:S(2)}, u32[]{:S(2)}) collective-permute-start(f32[232,1152]{1,0:T(8,128)} %north_message.1.after_ref), channel_id=1, source_target_pairs={{0,112},{16,0},{32,16},{48,32},{64,48},{80,64},{96,80},{112,96},{1... | collective-permute-start | bytes 3207176 | tf_op jit(solution)/shard_map/ppermute | solution.py:470
  5.4 1.7 %south_message.1.after_ref = f32[64,1152]{1,0:T(8,128)} custom-call(f32[144,1152]{1,0:T(8,128)} %e_ref.1, f32[144,1152]{1,0:T(8,128)} %u_ref.1, f32[144,1152]{1,0:T(8,128)} %v_ref.1, f32[144,1152]{1,0:T(8,128)} %b_ref.1, s32[4,144,1152]{2,1,0:T(8,128)} %m_ref.1, f32[232,1152]{1,0:T(8,128)} %north_message.1.after_ref), custom_call_target="tpu_custom_call" | custom-call | flops 80000 | bytes 600000 | tf_op jit(solution)/shard_map/south_message/pallas_call | solution.py:498
  7.1 4.6 %pack_rows.1 = f32[128,40,128]{2,1,0:T(8,128)} custom-call(s32[1,4]{1,0:T(1,128)} %bitcast.5, s32[4,256]{1,0:T(4,128)} %dest_ref.1, s32[4,256]{1,0:T(4,128)} %coarse_ref.1, f32[4,256,128]{2,1,0:T(8,128)} %vals_ref.1, f32[4,1,144]{2,1,0:T(1,128)} %panel_ref.1, f32[64,1152]{1,0:T(8,128)} %south_message.1.after_ref), custom_call_target="tpu_custom_call" | custom-call | flops 800000000 | bytes 3200000 | tf_op jit(solution)/shard_map/pack_rows/pallas_call | solution.py:513
  11.7 3.0 %collective-permute-done.south_ref = f32[64,1152]{1,0:T(8,128)S(1)} collective-permute-done((f32[64,1152]{1,0:T(8,128)}, f32[64,1152]{1,0:T(8,128)S(1)}, u32[]{:S(2)}, u32[]{:S(2)}) %collective-permute-start) | collective-permute-done | bytes 294944 | tf_op jit(solution)/shard_map/ppermute | solution.py:470
  14.7 3.5 %collective-permute-done.1.north_ref = f32[232,1152]{1,0:T(8,128)} collective-permute-done((f32[232,1152]{1,0:T(8,128)}, f32[232,1152]{1,0:T(8,128)}, u32[]{:S(2)}, u32[]{:S(2)}) %collective-permute-start.1) | collective-permute-done | bytes 1069088 | tf_op jit(solution)/shard_map/ppermute | solution.py:470
  18.2 11.6 %all-to-all-start = ((f32[128,40,128]{2,1,0:T(8,128)}), f32[128,40,128]{2,1,0:T(8,128)}, u32[]{:S(2)}, u32[]{:S(2)}) async-start(f32[128,40,128]{2,1,0:T(8,128)} %pack_rows.1), calls=%async_computation | async-start | bytes 5242880 | tf_op jit(solution)/shard_map/all_to_all | solution.py:523
  29.8 15.1 %prepare.1 = (f32[3,8,152,128]{3,2,1,0:T(8,128)}, f32[4,5,8,152,128]{4,3,2,1,0:T(8,128)}, bf16[4,256,1280]{2,1,0:T(8,128)(2,1)}, f32[8,3,200,128]{3,2,1,0:T(8,12...) custom-call(s32[2,4]{1,0:T(2,128)} %bitcast.2, f32[144,1152]{1,0:T(8,128)} %e_ref.1, f32[144,1152]{1,0:T(8,128)} %u_ref.1, ...), custom_call_target="tpu_custom_call" | custom-call | flops 60000000 | bytes 27000000 | tf_op jit(solution)/shard_map/prepare/pallas_call | solution.py:527
  45.0 5.1 %collective-permute-start.4 = (f32[3,152,128]{2,1,0:T(8,128)}, f32[3,152,128]{2,1,0:T(8,128)S(1)}, u32[]{:S(2)}, u32[]{:S(2)}) collective-permute-start(f32[3,152,128]{2,1,0:T(8,128)} %get-tuple-element.25), channel_id=1, source_target_pairs={{0,15},{1,0},{2,1},{3,2},{4,3},{5,4},{6,5},{7,6},{8,7},{9,8},{10,9... | collective-permute-start | bytes 700424 | tf_op jit(solution)/shard_map/ppermute | solution.py:470
  50.0 0.0 collective-permute-start.5
  50.0 14.8 %all-to-all-done.got_ref = f32[128,40,128]{2,1,0:T(8,128)} async-done(((f32[128,40,128]{2,1,0:T(8,128)}), f32[128,40,128]{2,1,0:T(8,128)}, u32[]{:S(2)}, u32[]{:S(2)}) %all-to-all-start) | async-done | bytes 2621472 | tf_op jit(solution)/shard_map/all_to_all | solution.py:523
  64.9 2.9 %receive_rows.1 = (f32[4,16,128]{2,1,0:T(8,128)}, f32[3,8,128]{2,1,0:T(8,128)}) custom-call(f32[128,40,128]{2,1,0:T(8,128)} %all-to-all-done.got_ref, f32[8,3,200,128]{3,2,1,0:T(8,128)} %get-tuple-element.23.after_ref.ends_ref), custom_call_target="tpu_custom_call" | custom-call | flops 300000000 | bytes 2700000 | tf_op jit(solution)/shard_map/receive_rows/pallas_call | solution.py:553
  67.8 0.0 collective-permute-start.3
  67.8 3.0 %collective-permute-start.2 = (f32[4,16,128]{2,1,0:T(8,128)}, f32[4,16,128]{2,1,0:T(8,128)S(1)}, u32[]{:S(2)}, u32[]{:S(2)}) collective-permute-start(f32[4,16,128]{2,1,0:T(8,128)} %get-tuple-element.24.after_ref), channel_id=1, source_target_pairs={{0,112},{16,0},{32,16},{48,32},{64,48},{80,64},{96,80},{112,96},{1... | collective-permute-start | bytes 98312 | tf_op jit(solution)/shard_map/ppermute | solution.py:470
  70.8 0.0 collective-permute-done.4.east_ref
  70.8 0.6 copy-done.4
  71.4 0.7 copy-done.2
  72.1 6.4 %side_strips.1 = (f32[3,2,152,128]{3,2,1,0:T(8,128)}, f32[4,5,2,152,128]{4,3,2,1,0:T(8,128)}) custom-call(s32[2,4]{1,0:T(2,128)} %bitcast.3, f32[8,3,200,128]{3,2,1,0:T(8,128)} %get-tuple-element.23.after_ref.ends_ref, f32[3,152,128]{2,1,0:T(8,128)} %copy-done.2, f32[152,128]{1,0:T(8,128)} %copy-done.4, f32[4,16,128]{2,1,0:T(8,128)} %get-tuple-element.24.after_ref), custom_call_target="tpu_custom_call" | custom-call | flops 12000000 | bytes 6000000 | tf_op jit(solution)/shard_map/side_strips/pallas_call | solution.py:564
  78.6 0.5 collective-permute-start.7
  79.1 4.9 %collective-permute-start.6 = (f32[4,32,128]{2,1,0:T(8,128)S(1)}, f32[4,32,128]{2,1,0:T(8,128)S(1)}, u32[]{:S(2)}, u32[]{:S(2)}) collective-permute-start(f32[4,32,128]{2,1,0:T(8,128)S(1)} %pad_maximum_fusion.own_ref), channel_id=1, source_target_pairs={{0,15},{1,0},{2,1},{3,2},{4,3},{5,4},{6,5},{7,6},{8,7},{9,8},{10,9... | collective-permute-start | bytes 196616 | tf_op jit(solution)/shard_map/ppermute | solution.py:470
  84.0 2.2 %collective-permute-done.7.west_ref = f32[4,32,128]{2,1,0:T(8,128)S(1)} collective-permute-done((f32[4,32,128]{2,1,0:T(8,128)S(1)}, f32[4,32,128]{2,1,0:T(8,128)S(1)}, u32[]{:S(2)}, u32[]{:S(2)}) %collective-permute-start.7) | collective-permute-done | bytes 65568 | tf_op jit(solution)/shard_map/ppermute | solution.py:470
  86.2 0.6 copy-done.5
  86.8 0.0 copy-done.6
  86.9 16.6 %steps.1 = (f32[144,1152]{1,0:T(8,128)}, f32[144,1152]{1,0:T(8,128)}, f32[144,1152]{1,0:T(8,128)}) custom-call(s32[2,4]{1,0:T(2,128)} %bitcast.4, f32[3,8,152,128]{3,2,1,0:T(8,128)} %get-tuple-element.21.mid_state, f32[3,2,152,128]{3,2,1,0:T(8,128)} %get-tuple-element.28.side_state, f32[4,5,8,152,128]{4,3,2,1,0:T(8,128)} %get-tuple-element.29.mid_hbm, ...), custom_call_target="tpu_custom_call" | custom-call | flops 400000000 | bytes 23000000 | tf_op jit(solution)/shard_map/steps/pallas_call | solution.py:587
  (18 shorter events, 0.1 us)
Async XLA Ops:
  3.1 15.1 %collective-permute-start.1 = (f32[232,1152]{1,0:T(8,128)}, f32[232,1152]{1,0:T(8,128)}, u32[]{:S(2)}, u32[]{:S(2)}) collective-permute-start(f32[232,1152]{1,0:T(8,128)} %north_message.1.after_ref), channel_id=1, source_target_pairs={{0,112},{16,0},{32,16},{48,32},{64,48},{80,64},{96,80},{112,96},{1... | collective-permute-start | bytes 3207176 | tf_op jit(solution)/shard_map/ppermute | solution.py:470
  7.1 7.6 %collective-permute-start = (f32[64,1152]{1,0:T(8,128)}, f32[64,1152]{1,0:T(8,128)S(1)}, u32[]{:S(2)}, u32[]{:S(2)}) collective-permute-start(f32[64,1152]{1,0:T(8,128)} %south_message.1.after_ref), channel_id=1, source_target_pairs={{0,16},{16,32},{32,48},{48,64},{64,80},{80,96},{96,112},{112,0},{1... | collective-permute-start | bytes 884744 | tf_op jit(solution)/shard_map/ppermute | solution.py:470
  14.7 15.2 %copy-start = (f32[64,1152]{1,0:T(8,128)}, f32[64,1152]{1,0:T(8,128)S(1)}, u32[]{:S(2)}) copy-start(f32[64,1152]{1,0:T(8,128)S(1)} %collective-permute-done.south_ref) | copy-start | bytes 884740
  18.2 46.7 %all-to-all-start = ((f32[128,40,128]{2,1,0:T(8,128)}), f32[128,40,128]{2,1,0:T(8,128)}, u32[]{:S(2)}, u32[]{:S(2)}) async-start(f32[128,40,128]{2,1,0:T(8,128)} %pack_rows.1), calls=%async_computation | async-start | bytes 5242880 | tf_op jit(solution)/shard_map/all_to_all | solution.py:523
  45.0 25.8 %collective-permute-start.4 = (f32[3,152,128]{2,1,0:T(8,128)}, f32[3,152,128]{2,1,0:T(8,128)S(1)}, u32[]{:S(2)}, u32[]{:S(2)}) collective-permute-start(f32[3,152,128]{2,1,0:T(8,128)} %get-tuple-element.25), channel_id=1, source_target_pairs={{0,15},{1,0},{2,1},{3,2},{4,3},{5,4},{6,5},{7,6},{8,7},{9,8},{10,9... | collective-permute-start | bytes 700424 | tf_op jit(solution)/shard_map/ppermute | solution.py:470
  50.0 20.7 %collective-permute-start.5 = (f32[152,128]{1,0:T(8,128)}, f32[152,128]{1,0:T(8,128)S(1)}, u32[]{:S(2)}, u32[]{:S(2)}) collective-permute-start(f32[152,128]{1,0:T(8,128)} %get-tuple-element.26), channel_id=1, source_target_pairs={{0,1},{1,2},{2,3},{3,4},{4,5},{5,6},{6,7},{7,8},{8,9},{9,10},{10,1... | collective-permute-start | bytes 233480 | tf_op jit(solution)/shard_map/ppermute | solution.py:470
  67.8 10.7 %copy-start.3 = (f32[4,16,128]{2,1,0:T(8,128)S(1)}, f32[4,16,128]{2,1,0:T(8,128)}, u32[]{:S(2)}) copy-start(f32[4,16,128]{2,1,0:T(8,128)} %get-tuple-element.24.after_ref) | copy-start | bytes 98308
  67.8 10.7 %collective-permute-start.3 = (f32[4,16,128]{2,1,0:T(8,128)}, f32[4,16,128]{2,1,0:T(8,128)S(1)}, u32[]{:S(2)}, u32[]{:S(2)}) collective-permute-start(f32[4,16,128]{2,1,0:T(8,128)} %get-tuple-element.24.after_ref), channel_id=1, source_target_pairs={{0,16},{16,32},{32,48},{48,64},{64,80},{80,96},{96,112},{112,0},{1... | collective-permute-start | bytes 98312 | tf_op jit(solution)/shard_map/ppermute | solution.py:470
  67.8 10.7 %collective-permute-start.2 = (f32[4,16,128]{2,1,0:T(8,128)}, f32[4,16,128]{2,1,0:T(8,128)S(1)}, u32[]{:S(2)}, u32[]{:S(2)}) collective-permute-start(f32[4,16,128]{2,1,0:T(8,128)} %get-tuple-element.24.after_ref), channel_id=1, source_target_pairs={{0,112},{16,0},{32,16},{48,32},{64,48},{80,64},{96,80},{112,96},{1... | collective-permute-start | bytes 98312 | tf_op jit(solution)/shard_map/ppermute | solution.py:470
  70.8 0.6 copy-start.4
  71.4 0.7 copy-start.2
  78.6 7.7 %copy-start.1 = (f32[4,32,128]{2,1,0:T(8,128)}, f32[4,32,128]{2,1,0:T(8,128)S(1)}, u32[]{:S(2)}) copy-start(f32[4,32,128]{2,1,0:T(8,128)S(1)} %pad_maximum_fusion.own_ref) | copy-start | bytes 196612
  78.6 7.7 %collective-permute-start.7 = (f32[4,32,128]{2,1,0:T(8,128)S(1)}, f32[4,32,128]{2,1,0:T(8,128)S(1)}, u32[]{:S(2)}, u32[]{:S(2)}) collective-permute-start(f32[4,32,128]{2,1,0:T(8,128)S(1)} %pad_maximum_fusion.own_ref), channel_id=1, source_target_pairs={{0,1},{1,2},{2,3},{3,4},{4,5},{5,6},{6,7},{7,8},{8,9},{9,10},{10,1... | collective-permute-start | bytes 196616 | tf_op jit(solution)/shard_map/ppermute | solution.py:470
  79.1 7.1 %collective-permute-start.6 = (f32[4,32,128]{2,1,0:T(8,128)S(1)}, f32[4,32,128]{2,1,0:T(8,128)S(1)}, u32[]{:S(2)}, u32[]{:S(2)}) collective-permute-start(f32[4,32,128]{2,1,0:T(8,128)S(1)} %pad_maximum_fusion.own_ref), channel_id=1, source_target_pairs={{0,15},{1,0},{2,1},{3,2},{4,3},{5,4},{6,5},{7,6},{8,7},{9,8},{10,9... | collective-permute-start | bytes 196616 | tf_op jit(solution)/shard_map/ppermute | solution.py:470
  86.2 0.6 copy-start.5
  86.2 0.7 copy-start.6
